TPU v7x, 32 devices: a whole 2x2x4 slice. The times are simulated.
32 devices in a mesh: member: 4 (over x, core), col: 8 (over z, y).
Axes of the slice: x: 2, y: 2, z: 4, core: 2. Of those that a mesh axis runs over, the one named last changes fastest.
Arguments:
- increment: bfloat16 [128, 137, 256], P(('member', 'col')), parts along dimension 0, may hold values from -6 to 6
- jacobian: bfloat16 [3072, 128, 137], P(('member', 'col')), parts along dimension 0, may hold values from -0.5 to 0.5
- innovation: bfloat16 [3072, 128, 256], P(('member', 'col')), parts along dimension 0, may hold values from -6 to 6
- inv_variance: float32 [128], replicated, may hold values from 0.25 to 4
- counts: int32 [3072, 256], P(('member', 'col')), parts along dimension 0, may hold values from 0 to 3
- owner: int32 [768, 1], replicated, may hold values from 0 to 7; in each aligned block of 96 rows (0 to 95, 96 to 191, ...) at most 24 rows name the same one
- local_block: int32 [768], replicated, may hold values from 0 to 3
Outputs:
- gradient: float32 [128, 137, 256], P(('member', 'col')), parts along dimension 0
There are 4 independent parts, one for each index of `member`. A program takes and returns all parts, laid end to end along the dimension named above; an argument that names none is the same for every part. Nothing has to cross between parts.
Inputs may be any that keep to these rules, and one draw needn't show every extreme that they name: `owner`: within the rows of one index of col (aligned blocks of 96 rows), no index of col appears more than 24 times, and some block reaches 24.
All inputs are finite; a program needn't handle non-finite values.
Results may differ from a plain program's by a relative error of at most 0.0012.
Values may be sent and summed in bfloat16 or wider, within the bound.
No kernel may reach another device: no remote copies, remote signals or barrier semaphores. Data moves between devices by JAX's collectives and lax.ppermute only.
A program may use at most 128 MiB of HBM per device.

v0:
```python
import jax
import jax.numpy as jnp
from jax import lax
from jax.sharding import PartitionSpec as P


def contributions(jac_part, inn_part, cnt_float, profile, inv_variance):
    evolved = jnp.einsum("bcl,blw->bcw", jac_part, profile, preferred_element_type=jnp.float32)
    weighted = (
        inv_variance[None, :, None]
        * cnt_float[:, None, :]
        * (evolved - inn_part.astype(jnp.float32))
    ).astype(jnp.bfloat16)
    return jnp.einsum("bcl,bcw->blw", jac_part, weighted, preferred_element_type=jnp.float32)


def body(increment, jacobian, innovation, inv_variance, counts, owner, local_block):
    obs_dev = jacobian.shape[0]
    blocks_dev = increment.shape[0]
    myself = lax.axis_index("col")
    all_owner = owner[:, 0]
    own_rows = lax.dynamic_slice_in_dim(all_owner, myself * obs_dev, obs_dev)
    own_local = lax.dynamic_slice_in_dim(local_block, myself * obs_dev, obs_dev)
    col_block = own_rows * blocks_dev + own_local
    whole = lax.all_gather(increment, "col", axis=0, tiled=True)
    adjoint = contributions(
        jacobian, innovation, counts.astype(jnp.float32), whole[col_block], inv_variance
    )
    count = blocks_dev * lax.axis_size("col")
    inside = (col_block >= 0) & (col_block < count)
    target = jnp.where(inside, col_block, count)
    summed = jax.ops.segment_sum(adjoint, target, num_segments=count + 1)
    return lax.psum_scatter(summed[:count], "col", scatter_dimension=0, tiled=True)


def solution(mesh):
    in_specs = (
        P(("member", "col"), None, None),
        P(("member", "col"), None, None),
        P(("member", "col"), None, None),
        P(),
        P(("member", "col"), None),
        P(),
        P(),
    )
    out_specs = P(("member", "col"), None, None)
    return jax.shard_map(body, mesh=mesh, in_specs=in_specs, out_specs=out_specs, check_vma=False)
```

profile of v0, /device:TPU:0, one launch (start us, length us, event | category | flops | bytes accessed | tf_op | source)
XLA Modules:
  0.0 229.6 jit_solution(5020921636024139461)
XLA Ops:
  6.5 0.0 copy-start
  6.5 0.0 all-gather.2.cloned.1.call-start
  6.5 1.8 copy.13
  8.4 0.0 all-gather.2.cloned.1.call-update
  8.4 0.0 reduce-scatter.2.cloned.1.call-start
  8.5 8.7 %copy.15 = bf16[96,128,256]{1,2,0:T(8,128)(2,1)} copy(bf16[96,128,256]{2,1,0:T(8,128)(2,1)} %param.9) | data formatting | bytes 12582912 | tf_op args[2]
  17.1 0.9 convert_element_type.9
  18.0 0.8 compare_select_fusion
  18.8 0.0 copy-start.1
  18.8 45.5 %all-gather.2.cloned.1.call-done = bf16[32,137,256]{2,1,0:T(8,128)(2,1)} async-done(((bf16[4,137,256]{2,1,0:T(8,128)(2,1)}), bf16[32,137,256]{2,1,0:T(8,128)(2,1)}) %all-gather.2.cloned.1.call-update) | async-done | bytes 2244624 | tf_op jit(solution)/shard_map/all_gather | solution.py:25
  64.4 8.0 %gather_fusion = bf16[96,137,256]{2,1,0:T(8,128)(2,1)} fusion(bf16[32,137,256]{2,1,0:T(8,128)(2,1)} %all-gather.2.cloned.1.call-done, s32[1024]{0:T(1024)S(1)} %pad_clamp_fusion), kind=kCustom, calls=%fused_computation | custom fusion | bytes 13468032 | tf_op jit(solution)/shard_map/gather | solution.py:27
  72.4 0.0 copy-done
  72.4 0.0 copy-done.1
  72.4 15.9 %convolution_bitcast_fusion = f32[96,137,256]{2,1,0:T(8,128)} fusion(bf16[96,128,256]{1,2,0:T(8,128)(2,1)} %copy.15, f32[96,256]{1,0:T(8,128)S(1)} %convert_element_type.9, f32[128]{0:T(128)S(1)} %copy-done.1, bf16[96,137,256]{2,1,0:T(8,128)(2,1)} %gather_fusion, bf16[96,128,137]{1,0,2:T(8,128)(2,1)S(1)} %copy-done), kind=kOutput, calls=%fused_computation.5 | convolution fusion | flops 1739587584 | bytes 29958656 | tf_op jit(solution)/shard_map/bcl,bcw->blw/dot_general | solution.py:14
  88.3 2.7 %broadcast_in_dim.13 = f32[33,137,256]{2,1,0:T(8,128)} broadcast(f32[]{:T(128)} %constant.7.clone.1), dimensions={} | broadcast | bytes 4629508 | tf_op jit(solution)/shard_map/broadcast_in_dim | solution.py:32
  91.0 30.6 %scatter_fusion = f32[33,137,256]{2,1,0:T(8,128)} fusion(f32[33,137,256]{2,1,0:T(8,128)} %broadcast_in_dim.13, s32[96]{0:T(128)S(1)} %and_select_fusion, f32[96,137,256]{2,1,0:T(8,128)} %convolution_bitcast_fusion), kind=kCustom, calls=%fused_computation.1 | custom fusion | flops 3366912 | bytes 40403328 | tf_op jit(solution)/shard_map/scatter-add | solution.py:32
  121.7 4.8 %slice.6 = f32[32,137,256]{2,1,0:T(8,128)} slice(f32[33,137,256]{2,1,0:T(8,128)} %scatter_fusion), slice={[0:32], [0:137], [0:256]} | slice | bytes 8978432 | tf_op jit(solution)/shard_map/slice | solution.py:33
  126.5 0.0 reduce-scatter.2.cloned.1.call-update
  126.5 94.0 %reduce-scatter.2.cloned.1.call-done = f32[4,137,256]{2,1,0:T(8,128)} async-done(((f32[32,137,256]{2,1,0:T(8,128)}), f32[4,137,256]{2,1,0:T(8,128)}) %reduce-scatter.2.cloned.1.call-update) | async-done | bytes 561168 | tf_op jit(solution)/shard_map/reduce_scatter | solution.py:33
  220.5 2.2 copy.18
  (2 shorter events, 0.0 us)
Async XLA Ops:
  6.5 65.9 %copy-start = (bf16[96,128,137]{1,0,2:T(8,128)(2,1)S(1)}, bf16[96,128,137]{1,0,2:T(8,128)(2,1)}, u32[]{:S(2)}) copy-start(bf16[96,128,137]{1,0,2:T(8,128)(2,1)} %param.8) | copy-start | bytes 10100740
  6.5 57.8 %all-gather.2.cloned.1.call-start = ((), (), s32[]{:S(2)}) async-start(), calls=%async_computation.1 | async-start | bytes 2654208 | tf_op jit(solution)/shard_map/all_gather | solution.py:25
  8.4 212.1 %reduce-scatter.2.cloned.1.call-start = ((), (), s32[]{:S(2)}) async-start(), calls=%async_computation.2 | async-start | bytes 5308416 | tf_op jit(solution)/shard_map/reduce_scatter | solution.py:33
  18.8 53.6 %copy-start.1 = (f32[128]{0:T(128)S(1)}, f32[128]{0:T(128)}, u32[]{:S(2)}) copy-start(f32[128]{0:T(128)} %param.10) | copy-start | bytes 1540
Sparse Core Ops, SparseCore 0:
  9.5 54.7 all-gather.1
  126.6 93.8 reduce-scatter.1
where the time goes:
time: 230 us
  waiting for transfers between devices  140 us (61%)
  other arithmetic  32.3 us (14%)
  local copies, waits for them, and re-layouts  28.3 us (12%)
  matrix products  15.9 us (7%)
  between operations  13.4 us (6%)
    reduce_scatter x1, waiting for transfers between devices, body(): lax.psum_scatter(summed[:count], 'col', scatter_dimension=0, tiled=True)  94 us
    all_gather x1, waiting for transfers between devices, body(): whole = lax.all_gather(increment, 'col', axis=0, tiled=True)  45.5 us
    scatter-add x1, other arithmetic, body(): summed = jax.ops.segment_sum(adjoint, target, num_segments=count + 1)  30.6 us
    dot_general x1, matrix products, contributions(): jnp.einsum('bcl,bcw->blw', jac_part, weighted, preferred_element_type=jnp...  15.9 us
    unnamed x6, local copies, waits for them, and re-layouts  10.5 us
    gather x1, local copies, waits for them, and re-layouts, body(): whole[col_block]  8.03 us
    slice x1, local copies, waits for them, and re-layouts, body(): summed[:count]  4.78 us
  transfers between devices with their start and end apart: 2, of which 2 were waited for; matrix products, arithmetic and copies ran while one was open for 5% of the time, Pallas kernels for 0%

commit v1 on v0

v1 whole, which is shorter than its diff:
```python
import functools

import jax
import jax.numpy as jnp
from jax import lax
from jax.experimental import pallas as pl
from jax.experimental.pallas import tpu as pltpu
from jax.sharding import PartitionSpec as P

TOP = 32000.0
LANES = 16
UNROLL = 4


def pack(x, rows):
    largest = jnp.maximum(jnp.max(jnp.abs(x), axis=0, keepdims=True), 1e-30)
    power = jnp.ceil(jnp.log2(largest))
    part = jnp.ceil(largest * jnp.exp2(14.0 - power))
    value = jnp.round(x * (TOP / (part * jnp.exp2(power - 14.0))))
    row = lax.broadcasted_iota(jnp.int32, x.shape, 0)
    value = jnp.where(row == rows, power, jnp.where(row == rows + 1, part, value))
    return value.astype(jnp.int32).astype(jnp.int16)


def unpack(coded, rows):
    value = coded.astype(jnp.int32).astype(jnp.float32)
    scale = value[rows + 1 : rows + 2] * jnp.exp2(value[rows : rows + 1] - 14.0) * (1.0 / TOP)
    row = lax.broadcasted_iota(jnp.int32, value.shape, 0)
    return jnp.where(row < rows, value * scale, 0.0)


def term_kernel(rows, n, inner, back, other, has_init, packed, table, inc, jac, inn, cnt, iv, *refs):
    out, acc = refs[-2:]
    blocks = inc.shape[0]
    outer = n // inner
    me = table[0]
    line, place = me // inner, lax.rem(me, inner)
    line = lax.rem(line + outer - back, outer)
    place = lax.rem(place + other, inner)
    holder = line * inner + place
    first, last = table[1 + holder], table[2 + holder]
    for l in range(blocks):
        acc[l] = unpack(refs[0][l], rows) if has_init else jnp.zeros(acc.shape[1:], jnp.float32)
    variance = iv[...]

    def step(i, carry):
        terms = []
        for u in range(UNROLL):
            p = first + i * UNROLL + u
            entry = table[2 + n + jnp.minimum(p, last - 1)]
            b, l = entry // blocks, lax.rem(entry, blocks)
            live = (p < last).astype(jnp.float32)
            evolved = lax.dot_general(
                jac[b], inc[l], (((0,), (0,)), ((), ())), preferred_element_type=jnp.float32
            )
            weight = variance * (cnt[pl.ds(b, 1), :].astype(jnp.float32) * live)
            weighted = (weight * (evolved - inn[b].astype(jnp.float32))).astype(jnp.bfloat16)
            terms.append((l, jnp.dot(jac[b], weighted, preferred_element_type=jnp.float32)))
        for l, t in terms:
            acc[l] += t
        return carry

    lax.fori_loop(0, (last - first + UNROLL - 1) // UNROLL, step, 0)
    for l in range(blocks):
        out[l] = pack(acc[l], rows) if packed else acc[l]


def term(rows, n, inner, back, other, packed, local, inc, init=None):
    table, jac, inn, cnt, iv = local
    smem = pl.BlockSpec(memory_space=pltpu.SMEM)
    vmem = pl.BlockSpec(memory_space=pltpu.VMEM)
    operands = [table, inc, jac, inn, cnt, iv] + ([] if init is None else [init])
    flops = 4 * (jac.shape[0] // n) * jac.shape[1] * jac.shape[2] * inc.shape[2]
    return pl.pallas_call(
        functools.partial(term_kernel, rows, n, inner, back, other, init is not None, packed),
        out_shape=jax.ShapeDtypeStruct(inc.shape, jnp.int16 if packed else jnp.float32),
        in_specs=[smem] + [vmem] * (len(operands) - 1),
        out_specs=vmem,
        scratch_shapes=[pltpu.VMEM(inc.shape, jnp.float32)],
        compiler_params=pltpu.CompilerParams(vmem_limit_bytes=24 * 2**20),
        cost_estimate=pl.CostEstimate(flops=flops, bytes_accessed=8 * 2**20, transcendentals=0),
    )(*operands)


def total_kernel(rows, own, *refs):
    out = refs[-1]
    for l in range(own.shape[0]):
        total = own[l]
        for coded in refs[:-1]:
            total = total + unpack(coded[l], rows)
        out[l] = total[:rows]


def total(rows, own, coded):
    vmem = pl.BlockSpec(memory_space=pltpu.VMEM)
    shape = (own.shape[0], rows, own.shape[2])
    return pl.pallas_call(
        functools.partial(total_kernel, rows),
        out_shape=jax.ShapeDtypeStruct(shape, jnp.float32),
        in_specs=[vmem] * (1 + len(coded)),
        out_specs=vmem,
        compiler_params=pltpu.CompilerParams(vmem_limit_bytes=24 * 2**20),
        cost_estimate=pl.CostEstimate(flops=2**20, bytes_accessed=2**22, transcendentals=0),
    )(own, *coded)


def sorted_table(owner, local_block, me, n, obs, blocks):
    rows = lax.dynamic_slice_in_dim(owner[:, 0], me * obs, obs)
    local = lax.dynamic_slice_in_dim(local_block, me * obs, obs)
    index = jnp.arange(obs, dtype=jnp.int32)
    key = (rows * blocks + local) * obs + index
    place = jnp.sum(key[None, :] < key[:, None], axis=1, dtype=jnp.int32)
    entry = index * blocks + local
    order = jnp.sum(jnp.where(place[None, :] == index[:, None], entry[None, :], 0), axis=1, dtype=jnp.int32)
    first = jnp.sum(rows[None, :] < jnp.arange(n + 1, dtype=jnp.int32)[:, None], axis=1, dtype=jnp.int32)
    return jnp.concatenate([me.astype(jnp.int32)[None], first, order])


def body(n, increment, jacobian, innovation, inv_variance, counts, owner, local_block):
    obs, channels, rows = jacobian.shape
    blocks = increment.shape[0]
    inner = 2 if n % 2 == 0 else 1
    outer = n // inner
    spare = -(rows + 2) % LANES + 2
    me = lax.axis_index("col")

    def along(x, shift):
        return lax.ppermute(
            x, "col", [(i, (i // inner + shift) % outer * inner + i % inner) for i in range(n)]
        )

    def across(x):
        return lax.ppermute(x, "col", [(i, i // inner * inner + (i + 1) % inner) for i in range(n)])

    inc = jnp.pad(increment, ((0, 0), (0, spare), (0, 0)))
    jac = jnp.pad(jnp.transpose(jacobian, (0, 2, 1)), ((0, 0), (0, spare), (0, 0)))
    table = sorted_table(owner, local_block, me, n, obs, blocks)
    local = (table, jac, innovation, counts, inv_variance[:, None])

    near = [inc]
    for back in range(1, outer):
        near.append(along(near[-1], 1))
    far = [across(x) for x in near] if inner > 1 else [None] * outer
    own = term(rows, n, inner, 0, 0, False, local, inc)
    arrived = []
    for back in range(outer):
        passed = None
        if inner > 1:
            passed = across(term(rows, n, inner, back, 1, True, local, far[back]))
        if back == 0:
            arrived += [] if passed is None else [passed]
        else:
            arrived.append(along(term(rows, n, inner, back, 0, True, local, near[back], passed), -back))
    return total(rows, own, arrived)


def solution(mesh):
    in_specs = (
        P(("member", "col"), None, None),
        P(("member", "col"), None, None),
        P(("member", "col"), None, None),
        P(),
        P(("member", "col"), None),
        P(),
        P(),
    )
    out_specs = P(("member", "col"), None, None)
    run = functools.partial(body, mesh.shape["col"])
    return jax.shard_map(run, mesh=mesh, in_specs=in_specs, out_specs=out_specs, check_vma=False)
```

time: 230 us -> 91.1 us (0.40)
  waiting for transfers between devices: 140 us -> 38.8 us
  other arithmetic: 32.3 us -> 1.24 us
  Pallas kernels: 0 us -> 23.7 us
  local copies, waits for them, and re-layouts: 28.3 us -> 12.1 us
  matrix products: 15.9 us -> 0 us
  starting transfers between devices: 0.04 us -> 14.7 us
  between operations: 13.4 us -> 0.15 us
    reduce_scatter x1 -> x0, waiting for transfers between devices: 94 us -> none  [body(): lax.psum_scatter(summed[:count], 'col', scatter_dimension=0, tiled=True)]
    all_gather x1 -> x0, waiting for transfers between devices: 45.5 us -> none  [body(): whole = lax.all_gather(increment, 'col', axis=0, tiled=True)]
    ppermute x0 -> x14, waiting for transfers between devices: none -> 38.8 us  [the longest x6 36.4 us: along(): lax.ppermute(x, 'col', [(i, (i // inner + shift) % outer * inner + i % in...]
    scatter-add x1 -> x0, other arithmetic: 30.6 us -> none  [body(): summed = jax.ops.segment_sum(adjoint, target, num_segments=count + 1)]
    pallas_call x0 -> x9, Pallas kernels: none -> 23.7 us  [the longest x8 23.3 us: term(): pl.pallas_call(functools.partial(term_kernel, rows, n, inner, back, other...]
    dot_general x1 -> x0, matrix products: 15.9 us -> none  [contributions(): jnp.einsum('bcl,bcw->blw', jac_part, weighted, preferred_element_type=jnp...]
    ppermute x0 -> x14, starting transfers between devices: none -> 14.7 us  [the longest x6 7.54 us: along(): lax.ppermute(x, 'col', [(i, (i // inner + shift) % outer * inner + i % in...]
    gather x1 -> x0, local copies, waits for them, and re-layouts: 8.03 us -> none  [body(): whole[col_block]]
  transfers between devices with their start and end apart: 2 -> 14, of which waited for: 2 -> 6; matrix products, arithmetic and copies ran while one was open for 5% -> 6% of each run, Pallas kernels for 0% -> 26%
where the time goes in v1:
time: 91.1 us; the launch traced here: 90.6 us
  waiting for transfers between devices  38.8 us (43%)
  Pallas kernels  23.7 us (26%)
  starting transfers between devices  14.7 us (16%)
  local copies, waits for them, and re-layouts  12.1 us (13%)
  other arithmetic  1.24 us (1%)
    ppermute x6, waiting for transfers between devices, along(): lax.ppermute(x, 'col', [(i, (i // inner + shift) % outer * inner + i % in...  36.4 us
    pallas_call x8, Pallas kernels, term(): pl.pallas_call(functools.partial(term_kernel, rows, n, inner, back, other...  23.3 us
    unnamed x14, local copies, waits for them, and re-layouts  9.16 us
    ppermute x6, starting transfers between devices, along(): lax.ppermute(x, 'col', [(i, (i // inner + shift) % outer * inner + i % in...  7.54 us
    ppermute x8, starting transfers between devices, across(): lax.ppermute(x, 'col', [(i, i // inner * inner + (i + 1) % inner) for i i...  7.14 us
    ppermute x8, waiting for transfers between devices, across(): lax.ppermute(x, 'col', [(i, i // inner * inner + (i + 1) % inner) for i i...  2.39 us
  transfers between devices with their start and end apart: 14, of which 6 were waited for; matrix products, arithmetic and copies ran while one was open for 6% of the time, Pallas kernels for 26%

profile of v1, /device:TPU:0, one launch (start us, length us, event | category | flops | bytes accessed | tf_op | source)
XLA Modules:
  0.0 90.6 jit_solution(14746860053980702996)
XLA Ops:
  0.0 1.0 %copy.19 = bf16[4,137,256]{2,1,0:T(8,128)(2,1)S(1)} copy(bf16[4,137,256]{2,0,1:T(4,128)(2,1)} %param.7) | data formatting | bytes 561152 | tf_op args[0]
  1.0 0.7 pad.8.inc
  1.7 3.0 %collective-permute-start.2 = (bf16[4,144,256]{2,1,0:T(8,128)(2,1)}, bf16[4,144,256]{2,1,0:T(8,128)(2,1)}, u32[]{:S(2)}, u32[]{:S(2)}) collective-permute-start(bf16[4,144,256]{2,1,0:T(8,128)(2,1)} %pad.8.inc), channel_id=1, source_target_pairs={{0,2},{1,3},{2,4},{3,5},{4,6},{5,7},{6,0},{7,1},{8,10},{9,11},{10,... | collective-permute-start | bytes 884744 | tf_op jit(solution)/shard_map/ppermute | solution.py:128
  4.8 9.3 %collective-permute-done.2.inc = bf16[4,144,256]{2,1,0:T(8,128)(2,1)} collective-permute-done((bf16[4,144,256]{2,1,0:T(8,128)(2,1)}, bf16[4,144,256]{2,1,0:T(8,128)(2,1)}, u32[]{:S(2)}, u32[]{:S(2)}) %collective-permute-start.2) | collective-permute-done | bytes 294944 | tf_op jit(solution)/shard_map/ppermute | solution.py:128
  14.1 0.0 collective-permute-start.6
  14.1 10.3 %collective-permute-done.6.inc = bf16[4,144,256]{2,1,0:T(8,128)(2,1)} collective-permute-done((bf16[4,144,256]{2,1,0:T(8,128)(2,1)}, bf16[4,144,256]{2,1,0:T(8,128)(2,1)}, u32[]{:S(2)}, u32[]{:S(2)}) %collective-permute-start.6) | collective-permute-done | bytes 294944 | tf_op jit(solution)/shard_map/ppermute | solution.py:128
  24.4 0.0 collective-permute-start.10
  24.4 1.3 %collective-permute-start = (bf16[4,144,256]{2,1,0:T(8,128)(2,1)}, bf16[4,144,256]{2,1,0:T(8,128)(2,1)}, u32[]{:S(2)}, u32[]{:S(2)}) collective-permute-start(bf16[4,144,256]{2,1,0:T(8,128)(2,1)} %pad.8.inc), channel_id=1, source_target_pairs={{0,1},{1,0},{2,3},{3,2},{4,5},{5,4},{6,7},{7,6},{8,9},{9,8},{10,11... | collective-permute-start | bytes 884744 | tf_op jit(solution)/shard_map/ppermute | solution.py:133
  25.7 0.8 iota_add_fusion
  26.5 0.2 convert_reduce_fusion
  26.6 0.8 collective-permute-start.3
  27.5 1.3 %collective-permute-start.7 = (bf16[4,144,256]{2,1,0:T(8,128)(2,1)}, bf16[4,144,256]{2,1,0:T(8,128)(2,1)}, u32[]{:S(2)}, u32[]{:S(2)}) collective-permute-start(bf16[4,144,256]{2,1,0:T(8,128)(2,1)} %collective-permute-done.6.inc), channel_id=1, source_target_pairs={{0,1},{1,0},{2,3},{3,2},{4,5},{5,4},{6,7},{7,6},{8,9},{9,8},{10,11... | collective-permute-start | bytes 884744 | tf_op jit(solution)/shard_map/ppermute | solution.py:133
  28.7 5.1 %collective-permute-done.10.inc = bf16[4,144,256]{2,1,0:T(8,128)(2,1)} collective-permute-done((bf16[4,144,256]{2,1,0:T(8,128)(2,1)}, bf16[4,144,256]{2,1,0:T(8,128)(2,1)}, u32[]{:S(2)}, u32[]{:S(2)}) %collective-permute-start.10) | collective-permute-done | bytes 294944 | tf_op jit(solution)/shard_map/ppermute | solution.py:128
  33.8 1.0 %collective-permute-start.11 = (bf16[4,144,256]{2,1,0:T(8,128)(2,1)}, bf16[4,144,256]{2,1,0:T(8,128)(2,1)}, u32[]{:S(2)}, u32[]{:S(2)}) collective-permute-start(bf16[4,144,256]{2,1,0:T(8,128)(2,1)} %collective-permute-done.10.inc), channel_id=1, source_target_pairs={{0,1},{1,0},{2,3},{3,2},{4,5},{5,4},{6,7},{7,6},{8,9},{9,8},{10,11... | collective-permute-start | bytes 884744 | tf_op jit(solution)/shard_map/ppermute | solution.py:133
  34.8 0.1 convert_reduce_fusion.1
  34.9 3.3 %copy.31 = bf16[96,128,137]{1,2,0:T(8,128)(2,1)S(1)} copy(bf16[96,128,137]{1,0,2:T(8,128)(2,1)} %param.8) | data formatting | bytes 6733824 | tf_op args[1]
  38.2 0.0 copy-start.3
  38.2 0.3 pad.9.jac
  38.5 0.4 copy-done.3
  38.9 0.7 copy.21.iv
  39.6 0.1 select_reduce_fusion
  39.7 0.1 pad_add_fusion.table
  39.8 1.2 %collective-permute-done.3.inc = bf16[4,144,256]{2,1,0:T(8,128)(2,1)} collective-permute-done((bf16[4,144,256]{2,1,0:T(8,128)(2,1)}, bf16[4,144,256]{2,1,0:T(8,128)(2,1)}, u32[]{:S(2)}, u32[]{:S(2)}) %collective-permute-start.3) | collective-permute-done | bytes 294944 | tf_op jit(solution)/shard_map/ppermute | solution.py:133
  41.0 0.0 copy-start
  41.0 2.8 %copy-done = bf16[96,128,256]{2,1,0:T(8,128)(2,1)S(1)} copy-done((bf16[96,128,256]{2,1,0:T(8,128)(2,1)S(1)}, bf16[96,128,256]{2,1,0:T(8,128)(2,1)}, u32[]{:S(2)}) %copy-start) | copy-done | bytes 6291480
  43.8 0.0 copy-start.1
  43.8 0.9 copy-done.1
  44.7 0.0 copy-start.2
  44.7 0.8 copy-done.2
  45.5 3.7 %shard_map.75 = s16[4,144,256]{2,1,0:T(8,128)(2,1)S(1)} custom-call(s32[106]{0:T(128)S(1)} %pad_add_fusion.table, bf16[4,144,256]{2,1,0:T(8,128)(2,1)} %collective-permute-done.3.inc, bf16[96,144,128]{2,1,0:T(8,128)(2,1)S(1)} %pad.9.jac, bf16[96,128,256]{2,1,0:T(8,128)(2,1)S(1)} %copy-done, s32[96,256]{1,0:T(8,128)S(1)} %copy-done.1, f32[128,1]{1,0:T(8,128)S(1)} %copy-done.2), custom_call_target="tpu_custom_call" | custom-call | flops 226492416 | bytes 8388608 | tf_op jit(solution)/shard_map/pallas_call | solution.py:74
  49.3 0.3 collective-permute-start.4
  49.6 0.0 collective-permute-done.7.inc
  49.6 4.3 %shard_map.77 = s16[4,144,256]{2,1,0:T(8,128)(2,1)S(1)} custom-call(s32[106]{0:T(128)S(1)} %pad_add_fusion.table, bf16[4,144,256]{2,1,0:T(8,128)(2,1)} %collective-permute-done.7.inc, bf16[96,144,128]{2,1,0:T(8,128)(2,1)S(1)} %pad.9.jac, bf16[96,128,256]{2,1,0:T(8,128)(2,1)S(1)} %copy-done, s32[96,256]{1,0:T(8,128)S(1)} %copy-done.1, f32[128,1]{1,0:T(8,128)S(1)} %copy-done.2), custom_call_target="tpu_custom_call" | custom-call | flops 226492416 | bytes 8388608 | tf_op jit(solution)/shard_map/pallas_call | solution.py:74
  53.8 0.3 collective-permute-start.8
  54.1 0.0 collective-permute-done.11.inc
  54.1 3.2 %shard_map.79 = s16[4,144,256]{2,1,0:T(8,128)(2,1)S(1)} custom-call(s32[106]{0:T(128)S(1)} %pad_add_fusion.table, bf16[4,144,256]{2,1,0:T(8,128)(2,1)} %collective-permute-done.11.inc, bf16[96,144,128]{2,1,0:T(8,128)(2,1)S(1)} %pad.9.jac, bf16[96,128,256]{2,1,0:T(8,128)(2,1)S(1)} %copy-done, s32[96,256]{1,0:T(8,128)S(1)} %copy-done.1, f32[128,1]{1,0:T(8,128)S(1)} %copy-done.2), custom_call_target="tpu_custom_call" | custom-call | flops 226492416 | bytes 8388608 | tf_op jit(solution)/shard_map/pallas_call | solution.py:74
  57.4 0.8 collective-permute-start.12
  58.2 0.0 collective-permute-done.inc
  58.2 2.2 %shard_map.74 = s16[4,144,256]{2,1,0:T(8,128)(2,1)S(1)} custom-call(s32[106]{0:T(128)S(1)} %pad_add_fusion.table, bf16[4,144,256]{2,1,0:T(8,128)(2,1)} %collective-permute-done.inc, bf16[96,144,128]{2,1,0:T(8,128)(2,1)S(1)} %pad.9.jac, bf16[96,128,256]{2,1,0:T(8,128)(2,1)S(1)} %copy-done, s32[96,256]{1,0:T(8,128)S(1)} %copy-done.1, f32[128,1]{1,0:T(8,128)S(1)} %copy-done.2), custom_call_target="tpu_custom_call" | custom-call | flops 226492416 | bytes 8388608 | tf_op jit(solution)/shard_map/pallas_call | solution.py:74
  60.4 1.3 %collective-permute-start.1 = (s16[4,144,256]{2,1,0:T(8,128)(2,1)S(1)}, s16[4,144,256]{2,1,0:T(8,128)(2,1)S(1)}, u32[]{:S(2)}, u32[]{:S(2)}) collective-permute-start(s16[4,144,256]{2,1,0:T(8,128)(2,1)S(1)} %shard_map.74), channel_id=1, source_target_pairs={{0,1},{1,0},{2,3},{3,2},{4,5},{5,4},{6,7},{7,6},{8,9},{9,8},{10,11... | collective-permute-start | bytes 884744 | tf_op jit(solution)/shard_map/ppermute | solution.py:133
  61.7 0.0 collective-permute-done.4.refs_0_
  61.7 2.7 %shard_map.76 = s16[4,144,256]{2,1,0:T(8,128)(2,1)S(1)} custom-call(s32[106]{0:T(128)S(1)} %pad_add_fusion.table, bf16[4,144,256]{2,1,0:T(8,128)(2,1)} %collective-permute-done.2.inc, bf16[96,144,128]{2,1,0:T(8,128)(2,1)S(1)} %pad.9.jac, bf16[96,128,256]{2,1,0:T(8,128)(2,1)S(1)} %copy-done, s32[96,256]{1,0:T(8,128)S(1)} %copy-done.1, ...), custom_call_target="tpu_custom_call" | custom-call | flops 226492416 | bytes 8388608 | tf_op jit(solution)/shard_map/pallas_call | solution.py:74
  64.5 3.9 %collective-permute-start.5 = (s16[4,144,256]{2,1,0:T(8,128)(2,1)S(1)}, s16[4,144,256]{2,1,0:T(8,128)(2,1)S(1)}, u32[]{:S(2)}, u32[]{:S(2)}) collective-permute-start(s16[4,144,256]{2,1,0:T(8,128)(2,1)S(1)} %shard_map.76), channel_id=1, source_target_pairs={{0,6},{1,7},{2,0},{3,1},{4,2},{5,3},{6,4},{7,5},{8,14},{9,15},{10,... | collective-permute-start | bytes 884744 | tf_op jit(solution)/shard_map/ppermute | solution.py:128
  68.3 0.0 collective-permute-done.8.refs_0_
  68.3 0.0 slice-start
  68.3 2.9 %shard_map.78 = s16[4,144,256]{2,1,0:T(8,128)(2,1)S(1)} custom-call(s32[106]{0:T(128)S(1)} %pad_add_fusion.table, bf16[4,144,256]{2,1,0:T(8,128)(2,1)} %collective-permute-done.6.inc, bf16[96,144,128]{2,1,0:T(8,128)(2,1)S(1)} %pad.9.jac, bf16[96,128,256]{2,1,0:T(8,128)(2,1)S(1)} %copy-done, s32[96,256]{1,0:T(8,128)S(1)} %copy-done.1, ...), custom_call_target="tpu_custom_call" | custom-call | flops 226492416 | bytes 8388608 | tf_op jit(solution)/shard_map/pallas_call | solution.py:74
  71.2 0.0 slice-start.1
  71.2 0.1 collective-permute-start.9
  71.3 1.2 %collective-permute-done.12.refs_0_ = s16[4,144,256]{2,1,0:T(8,128)(2,1)S(1)} collective-permute-done((s16[4,144,256]{2,1,0:T(8,128)(2,1)S(1)}, s16[4,144,256]{2,1,0:T(8,128)(2,1)S(1)}, u32[]{:S(2)}, u32[]{:S(2)}) %collective-permute-start.12) | collective-permute-done | bytes 294944 | tf_op jit(solution)/shard_map/ppermute | solution.py:133
  72.5 2.2 %shard_map.80 = s16[4,144,256]{2,1,0:T(8,128)(2,1)S(1)} custom-call(s32[106]{0:T(128)S(1)} %pad_add_fusion.table, bf16[4,144,256]{2,1,0:T(8,128)(2,1)} %collective-permute-done.10.inc, bf16[96,144,128]{2,1,0:T(8,128)(2,1)S(1)} %pad.9.jac, bf16[96,128,256]{2,1,0:T(8,128)(2,1)S(1)} %copy-done, s32[96,256]{1,0:T(8,128)S(1)} %copy-done.1, ...), custom_call_target="tpu_custom_call" | custom-call | flops 226492416 | bytes 8388608 | tf_op jit(solution)/shard_map/pallas_call | solution.py:74
  74.7 0.6 collective-permute-start.13
  75.3 0.0 slice-done
  75.3 0.0 slice-done.1
  75.3 2.1 %shard_map.73.own = f32[4,144,256]{2,1,0:T(8,128)S(1)} custom-call(s32[106]{0:T(128)S(1)} %pad_add_fusion.table, bf16[4,144,256]{2,1,0:T(8,128)(2,1)} %pad.8.inc, bf16[96,144,128]{2,1,0:T(8,128)(2,1)S(1)} %pad.9.jac, bf16[96,128,256]{2,1,0:T(8,128)(2,1)S(1)} %bitcast.9, s32[96,256]{1,0:T(8,128)S(1)} %copy-done.1, f32[128,1]{1,0:T(8,128)S(1)} %copy-done.2), custom_call_target="tpu_custom_call" | custom-call | flops 226492416 | bytes 8388608 | tf_op jit(solution)/shard_map/pallas_call | solution.py:74
  77.4 0.0 collective-permute-done.1.refs_0_
  77.4 0.0 collective-permute-done.5.refs_1_
  77.4 11.7 %collective-permute-done.9.refs_2_ = s16[4,144,256]{2,1,0:T(8,128)(2,1)S(1)} collective-permute-done((s16[4,144,256]{2,1,0:T(8,128)(2,1)S(1)}, s16[4,144,256]{2,1,0:T(8,128)(2,1)S(1)}, u32[]{:S(2)}, u32[]{:S(2)}) %collective-permute-start.9) | collective-permute-done | bytes 294944 | tf_op jit(solution)/shard_map/ppermute | solution.py:128
  89.1 0.0 collective-permute-done.13.refs_3_
  89.1 0.3 shard_map.81
  89.4 1.2 %copy.29 = f32[4,137,256]{2,0,1:T(4,128)} copy(f32[4,137,256]{2,1,0:T(8,128)S(1)} %shard_map.81) | data formatting | bytes 1122304 | tf_op jit(solution)/shard_map/pallas_call | solution.py:97
  (1 shorter events, 0.0 us)
Async XLA Ops:
  1.7 12.4 %collective-permute-start.2 = (bf16[4,144,256]{2,1,0:T(8,128)(2,1)}, bf16[4,144,256]{2,1,0:T(8,128)(2,1)}, u32[]{:S(2)}, u32[]{:S(2)}) collective-permute-start(bf16[4,144,256]{2,1,0:T(8,128)(2,1)} %pad.8.inc), channel_id=1, source_target_pairs={{0,2},{1,3},{2,4},{3,5},{4,6},{5,7},{6,0},{7,1},{8,10},{9,11},{10,... | collective-permute-start | bytes 884744 | tf_op jit(solution)/shard_map/ppermute | solution.py:128
  14.1 10.3 %collective-permute-start.6 = (bf16[4,144,256]{2,1,0:T(8,128)(2,1)}, bf16[4,144,256]{2,1,0:T(8,128)(2,1)}, u32[]{:S(2)}, u32[]{:S(2)}) collective-permute-start(bf16[4,144,256]{2,1,0:T(8,128)(2,1)} %collective-permute-done.2.inc), channel_id=1, source_target_pairs={{0,2},{1,3},{2,4},{3,5},{4,6},{5,7},{6,0},{7,1},{8,10},{9,11},{10,... | collective-permute-start | bytes 884744 | tf_op jit(solution)/shard_map/ppermute | solution.py:128
  24.4 9.4 %collective-permute-start.10 = (bf16[4,144,256]{2,1,0:T(8,128)(2,1)}, bf16[4,144,256]{2,1,0:T(8,128)(2,1)}, u32[]{:S(2)}, u32[]{:S(2)}) collective-permute-start(bf16[4,144,256]{2,1,0:T(8,128)(2,1)} %collective-permute-done.6.inc), channel_id=1, source_target_pairs={{0,2},{1,3},{2,4},{3,5},{4,6},{5,7},{6,0},{7,1},{8,10},{9,11},{10,... | collective-permute-start | bytes 884744 | tf_op jit(solution)/shard_map/ppermute | solution.py:128
  24.4 33.8 %collective-permute-start = (bf16[4,144,256]{2,1,0:T(8,128)(2,1)}, bf16[4,144,256]{2,1,0:T(8,128)(2,1)}, u32[]{:S(2)}, u32[]{:S(2)}) collective-permute-start(bf16[4,144,256]{2,1,0:T(8,128)(2,1)} %pad.8.inc), channel_id=1, source_target_pairs={{0,1},{1,0},{2,3},{3,2},{4,5},{5,4},{6,7},{7,6},{8,9},{9,8},{10,11... | collective-permute-start | bytes 884744 | tf_op jit(solution)/shard_map/ppermute | solution.py:133
  26.6 14.4 %collective-permute-start.3 = (bf16[4,144,256]{2,1,0:T(8,128)(2,1)}, bf16[4,144,256]{2,1,0:T(8,128)(2,1)}, u32[]{:S(2)}, u32[]{:S(2)}) collective-permute-start(bf16[4,144,256]{2,1,0:T(8,128)(2,1)} %collective-permute-done.2.inc), channel_id=1, source_target_pairs={{0,1},{1,0},{2,3},{3,2},{4,5},{5,4},{6,7},{7,6},{8,9},{9,8},{10,11... | collective-permute-start | bytes 884744 | tf_op jit(solution)/shard_map/ppermute | solution.py:133
  27.5 22.1 %collective-permute-start.7 = (bf16[4,144,256]{2,1,0:T(8,128)(2,1)}, bf16[4,144,256]{2,1,0:T(8,128)(2,1)}, u32[]{:S(2)}, u32[]{:S(2)}) collective-permute-start(bf16[4,144,256]{2,1,0:T(8,128)(2,1)} %collective-permute-done.6.inc), channel_id=1, source_target_pairs={{0,1},{1,0},{2,3},{3,2},{4,5},{5,4},{6,7},{7,6},{8,9},{9,8},{10,11... | collective-permute-start | bytes 884744 | tf_op jit(solution)/shard_map/ppermute | solution.py:133
  33.8 20.3 %collective-permute-start.11 = (bf16[4,144,256]{2,1,0:T(8,128)(2,1)}, bf16[4,144,256]{2,1,0:T(8,128)(2,1)}, u32[]{:S(2)}, u32[]{:S(2)}) collective-permute-start(bf16[4,144,256]{2,1,0:T(8,128)(2,1)} %collective-permute-done.10.inc), channel_id=1, source_target_pairs={{0,1},{1,0},{2,3},{3,2},{4,5},{5,4},{6,7},{7,6},{8,9},{9,8},{10,11... | collective-permute-start | bytes 884744 | tf_op jit(solution)/shard_map/ppermute | solution.py:133
  38.2 0.7 copy-start.3
  41.0 2.8 %copy-start = (bf16[96,128,256]{2,1,0:T(8,128)(2,1)S(1)}, bf16[96,128,256]{2,1,0:T(8,128)(2,1)}, u32[]{:S(2)}) copy-start(bf16[96,128,256]{2,1,0:T(8,128)(2,1)} %inn.15) | copy-start | bytes 18874372
  43.8 0.9 copy-start.1
  44.7 0.8 copy-start.2
  49.3 12.4 %collective-permute-start.4 = (s16[4,144,256]{2,1,0:T(8,128)(2,1)S(1)}, s16[4,144,256]{2,1,0:T(8,128)(2,1)S(1)}, u32[]{:S(2)}, u32[]{:S(2)}) collective-permute-start(s16[4,144,256]{2,1,0:T(8,128)(2,1)S(1)} %shard_map.75), channel_id=1, source_target_pairs={{0,1},{1,0},{2,3},{3,2},{4,5},{5,4},{6,7},{7,6},{8,9},{9,8},{10,11... | collective-permute-start | bytes 884744 | tf_op jit(solution)/shard_map/ppermute | solution.py:133
  53.8 14.5 %collective-permute-start.8 = (s16[4,144,256]{2,1,0:T(8,128)(2,1)S(1)}, s16[4,144,256]{2,1,0:T(8,128)(2,1)S(1)}, u32[]{:S(2)}, u32[]{:S(2)}) collective-permute-start(s16[4,144,256]{2,1,0:T(8,128)(2,1)S(1)} %shard_map.77), channel_id=1, source_target_pairs={{0,1},{1,0},{2,3},{3,2},{4,5},{5,4},{6,7},{7,6},{8,9},{9,8},{10,11... | collective-permute-start | bytes 884744 | tf_op jit(solution)/shard_map/ppermute | solution.py:133
  57.4 15.1 %collective-permute-start.12 = (s16[4,144,256]{2,1,0:T(8,128)(2,1)S(1)}, s16[4,144,256]{2,1,0:T(8,128)(2,1)S(1)}, u32[]{:S(2)}, u32[]{:S(2)}) collective-permute-start(s16[4,144,256]{2,1,0:T(8,128)(2,1)S(1)} %shard_map.79), channel_id=1, source_target_pairs={{0,1},{1,0},{2,3},{3,2},{4,5},{5,4},{6,7},{7,6},{8,9},{9,8},{10,11... | collective-permute-start | bytes 884744 | tf_op jit(solution)/shard_map/ppermute | solution.py:133
  60.4 17.0 %collective-permute-start.1 = (s16[4,144,256]{2,1,0:T(8,128)(2,1)S(1)}, s16[4,144,256]{2,1,0:T(8,128)(2,1)S(1)}, u32[]{:S(2)}, u32[]{:S(2)}) collective-permute-start(s16[4,144,256]{2,1,0:T(8,128)(2,1)S(1)} %shard_map.74), channel_id=1, source_target_pairs={{0,1},{1,0},{2,3},{3,2},{4,5},{5,4},{6,7},{7,6},{8,9},{9,8},{10,11... | collective-permute-start | bytes 884744 | tf_op jit(solution)/shard_map/ppermute | solution.py:133
  64.5 12.9 %collective-permute-start.5 = (s16[4,144,256]{2,1,0:T(8,128)(2,1)S(1)}, s16[4,144,256]{2,1,0:T(8,128)(2,1)S(1)}, u32[]{:S(2)}, u32[]{:S(2)}) collective-permute-start(s16[4,144,256]{2,1,0:T(8,128)(2,1)S(1)} %shard_map.76), channel_id=1, source_target_pairs={{0,6},{1,7},{2,0},{3,1},{4,2},{5,3},{6,4},{7,5},{8,14},{9,15},{10,... | collective-permute-start | bytes 884744 | tf_op jit(solution)/shard_map/ppermute | solution.py:128
  68.3 6.9 %slice-start = ((s8[6291456]{0:T(1024)(128)(4,1)}), s8[4194304]{0:T(1024)(128)(4,1)S(1)}, s32[]{:S(2)}) async-start(s8[6291456]{0:T(1024)(128)(4,1)} %bitcast.8), calls=%async_computation | async-start | bytes 8388608
  71.2 4.1 %slice-start.1 = ((s8[6291456]{0:T(1024)(128)(4,1)}), s8[2097152]{0:T(1024)(128)(4,1)S(1)}, s32[]{:S(2)}) async-start(s8[6291456]{0:T(1024)(128)(4,1)} %bitcast.8), calls=%async_computation.1 | async-start | bytes 4194304
  71.2 17.9 %collective-permute-start.9 = (s16[4,144,256]{2,1,0:T(8,128)(2,1)S(1)}, s16[4,144,256]{2,1,0:T(8,128)(2,1)S(1)}, u32[]{:S(2)}, u32[]{:S(2)}) collective-permute-start(s16[4,144,256]{2,1,0:T(8,128)(2,1)S(1)} %shard_map.78), channel_id=1, source_target_pairs={{0,4},{1,5},{2,6},{3,7},{4,0},{5,1},{6,2},{7,3},{8,12},{9,13},{10,... | collective-permute-start | bytes 884744 | tf_op jit(solution)/shard_map/ppermute | solution.py:128
  74.7 14.4 %collective-permute-start.13 = (s16[4,144,256]{2,1,0:T(8,128)(2,1)S(1)}, s16[4,144,256]{2,1,0:T(8,128)(2,1)S(1)}, u32[]{:S(2)}, u32[]{:S(2)}) collective-permute-start(s16[4,144,256]{2,1,0:T(8,128)(2,1)S(1)} %shard_map.80), channel_id=1, source_target_pairs={{0,2},{1,3},{2,4},{3,5},{4,6},{5,7},{6,0},{7,1},{8,10},{9,11},{10,... | collective-permute-start | bytes 884744 | tf_op jit(solution)/shard_map/ppermute | solution.py:128

commit v2 on v1

v2 whole, which is shorter than its diff:
```python
import functools

import jax
import jax.numpy as jnp
import numpy as np
from jax import lax
from jax.experimental import pallas as pl
from jax.experimental.pallas import tpu as pltpu
from jax.sharding import PartitionSpec as P

TOP = 32000.0
LANES = 16
UNROLL = 6


def pack(x, rows):
    largest = jnp.maximum(jnp.max(jnp.abs(x), axis=0, keepdims=True), 1e-30)
    power = jnp.ceil(jnp.log2(largest))
    part = jnp.ceil(largest * jnp.exp2(14.0 - power))
    value = jnp.round(x * (TOP / (part * jnp.exp2(power - 14.0))))
    row = lax.broadcasted_iota(jnp.int32, x.shape, 0)
    value = jnp.where(row == rows, power, jnp.where(row == rows + 1, part, value))
    return value.astype(jnp.int32).astype(jnp.int16)


def unpack(coded, rows):
    value = coded.astype(jnp.int32).astype(jnp.float32)
    scale = value[rows + 1 : rows + 2] * jnp.exp2(value[rows : rows + 1] - 14.0) * (1.0 / TOP)
    return value * scale


def term_kernel(n, which, count, packed, table, inc, jac, inn, cnt, iv, *refs):
    out, acc = refs[-2:]
    blocks, rows = inc.shape[:2]
    first, last = table[which], table[n + which]
    for l in range(blocks):
        acc[l] = jnp.zeros(acc.shape[1:], jnp.float32)
        if count:
            acc[l, :rows] = sum(unpack(coded[l], rows)[:rows] for coded in refs[:count])
    variance = iv[:, :1]

    def step(i, carry):
        terms = []
        for u in range(UNROLL):
            p = first + i * UNROLL + u
            entry = table[2 * n + jnp.minimum(p, last - 1)]
            b, l = entry // blocks, lax.rem(entry, blocks)
            live = (p < last).astype(jnp.float32)
            evolved = lax.dot_general(
                jac[b], inc[l], (((0,), (0,)), ((), ())), preferred_element_type=jnp.float32
            )
            weight = variance * (cnt[pl.ds(b, 1), :].astype(jnp.float32) * live)
            weighted = (weight * (evolved - inn[b].astype(jnp.float32))).astype(jnp.bfloat16)
            terms.append((l, jnp.dot(jac[b], weighted, preferred_element_type=jnp.float32)))
        for l, t in terms:
            acc[l, :rows] += t
        return carry

    lax.fori_loop(0, (last - first + UNROLL - 1) // UNROLL, step, 0)
    for l in range(blocks):
        out[l] = pack(acc[l], rows) if packed else acc[l, :rows]


def term(padded, n, which, packed, local, inc, *coded):
    table, jac, inn, cnt, iv = local
    smem = pl.BlockSpec(memory_space=pltpu.SMEM)
    vmem = pl.BlockSpec(memory_space=pltpu.VMEM)
    operands = [table, inc, jac, inn, cnt, iv, *coded]

    def shape(dtype, rows):
        return jax.ShapeDtypeStruct((inc.shape[0], rows, inc.shape[2]), dtype)

    return pl.pallas_call(
        functools.partial(term_kernel, n, which, len(coded), packed),
        out_shape=shape(jnp.int16, padded) if packed else shape(jnp.float32, inc.shape[1]),
        in_specs=[smem] + [vmem] * (len(operands) - 1),
        out_specs=vmem,
        scratch_shapes=[pltpu.VMEM((inc.shape[0], padded, inc.shape[2]), jnp.float32)],
        compiler_params=pltpu.CompilerParams(vmem_limit_bytes=16 * 2**20),
        cost_estimate=pl.CostEstimate(flops=2**20, bytes_accessed=8 * 2**20, transcendentals=0),
    )(*operands)


def order(outer):
    end = outer - 1
    if outer < 4:
        todo = [(kind, k) for k in range(1, outer) for kind in "zAy"]
        todo += [(kind, 0) for kind in "OBPs"]
        todo += [(kind, k) for k in range(1, outer) for kind in "BPs"]
        return todo + [(kind, k) for k in range(1, outer) for kind in "STr"]
    todo = [("z", end), ("A", 1), ("O", 0), ("z", 2), ("y", 1), ("B", 0), ("w", end), ("P", 0)]
    for k in range(2, end):
        todo += [("A", k), ("z", k + 1), ("y", k)] if k + 1 < end else [("A", k), ("y", k)]
        todo += [(kind, k - 1) for kind in "BPs"]
        if k > 3:
            todo += [(kind, k - 3) for kind in "STr"]
    todo += [(kind, end - 1) for kind in "BPs"]
    todo += [(kind, end) for kind in "ABPs"]
    todo += [(kind, k) for k in range(max(end - 3, 1), end) for kind in "STr"]
    return todo + [("s", 0), ("S", end), ("T", end), ("r", end)]


def at_hand_kernel(jac, inn, iv, turned, copied, column, whole, jac_sem, inn_sem):
    count = jac_sem.shape[0]
    some = jac.shape[1] // count
    copy = pltpu.make_async_copy(inn, copied, inn_sem)
    parts = [
        pltpu.make_async_copy(jac.at[:, pl.ds(i * some, some)], whole.at[:, pl.ds(i * some, some)], jac_sem.at[i])
        for i in range(count)
    ]
    for part in parts:
        part.start()
    copy.start()
    column[...] = jnp.swapaxes(jnp.broadcast_to(iv[...], column.shape[::-1]), 0, 1)
    for i, part in enumerate(parts):
        part.wait()
        turned[pl.ds(i * some, some)] = jnp.swapaxes(whole[:, pl.ds(i * some, some)], 0, 1)
    copy.wait()


def at_hand(jacobian, innovation, inv_variance):
    obs, channels, levels = jacobian.shape
    some = LANES if obs % LANES == 0 else obs
    hbm, vmem = pl.BlockSpec(memory_space=pltpu.HBM), pl.BlockSpec(memory_space=pltpu.VMEM)
    return pl.pallas_call(
        at_hand_kernel,
        out_shape=(
            pltpu.VMEM((obs, levels, channels), jacobian.dtype),
            pltpu.VMEM(innovation.shape, innovation.dtype),
            pltpu.VMEM((channels, 8), inv_variance.dtype),
        ),
        in_specs=[hbm, hbm, vmem],
        out_specs=(vmem, vmem, vmem),
        scratch_shapes=[
            pltpu.VMEM((levels, obs, channels), jacobian.dtype),
            pltpu.SemaphoreType.DMA((obs // some,)),
            pltpu.SemaphoreType.DMA(()),
        ],
        compiler_params=pltpu.CompilerParams(vmem_limit_bytes=24 * 2**20),
        cost_estimate=pl.CostEstimate(flops=2**20, bytes_accessed=10 * 2**20, transcendentals=0),
    )(
        pltpu.with_memory_space_constraint(jnp.transpose(jacobian, (2, 0, 1)), pltpu.HBM),
        pltpu.with_memory_space_constraint(innovation, pltpu.HBM),
        inv_variance[None, :],
    )


def total_kernel(own, *refs):
    out = refs[-1]
    rows = own.shape[1]
    for l in range(own.shape[0]):
        total = own[l]
        for coded in refs[:-1]:
            total = total + unpack(coded[l], rows)[:rows]
        out[:, l, :] = total


def total(own, coded):
    vmem = pl.BlockSpec(memory_space=pltpu.VMEM)
    blocks, rows, columns = own.shape
    levels_first = pl.pallas_call(
        total_kernel,
        out_shape=jax.ShapeDtypeStruct((rows, blocks, columns), own.dtype),
        in_specs=[vmem] * (1 + len(coded)),
        out_specs=vmem,
        compiler_params=pltpu.CompilerParams(vmem_limit_bytes=16 * 2**20),
        cost_estimate=pl.CostEstimate(flops=2**20, bytes_accessed=8 * 2**20, transcendentals=0),
    )(own, *coded)
    return jnp.transpose(levels_first, (1, 0, 2))


def folded(count):
    return list(range(0, 1)) + list(range(1, count, 2)) + list(range((count - 1) // 2 * 2, 0, -2))


def after(x, gate):
    return lax.optimization_barrier((x, gate))[0]


def sorted_table(owner, local_block, me, holders, obs, blocks):
    rows = lax.dynamic_slice_in_dim(owner[:, 0], me * obs, obs)
    local = lax.dynamic_slice_in_dim(local_block, me * obs, obs)
    index = jnp.arange(obs, dtype=jnp.int32)
    key = (rows * blocks + local) * obs + index
    place = jnp.sum(key[None, :] < key[:, None], axis=1, dtype=jnp.int32)
    entry = index * blocks + local
    order = jnp.sum(jnp.where(place[None, :] == index[:, None], entry[None, :], 0), axis=1, dtype=jnp.int32)
    first = jnp.sum(rows[None, :] < holders[:, None], axis=1, dtype=jnp.int32)
    last = jnp.sum(rows[None, :] <= holders[:, None], axis=1, dtype=jnp.int32)
    return jnp.concatenate([first, last, order])


def body(n, increment, jacobian, innovation, inv_variance, counts, owner, local_block):
    obs, channels, rows = jacobian.shape
    blocks = increment.shape[0]
    inner = 2
    outer = n // inner
    padded = -(-(rows + 2) // LANES) * LANES
    me = lax.axis_index("col")

    ring = folded(outer)

    def along(x, shift):
        lines = [(ring[p], ring[(p + shift) % outer]) for p in range(outer)]
        return lax.ppermute(x, "col", [(a * inner + r, b * inner + r) for a, b in lines for r in range(inner)])

    def across(x):
        return lax.ppermute(x, "col", [(i, i // inner * inner + (i + 1) % inner) for i in range(n)])

    inc = increment
    seat = {line: p for p, line in enumerate(ring)}
    holders = np.array(
        [
            [ring[(seat[i // inner] - back) % outer] * inner + (i + other) % inner for back in range(outer) for other in range(inner)]
            for i in range(n)
        ],
        np.int32,
    )
    table = sorted_table(owner, local_block, me, jnp.asarray(holders)[me], obs, blocks)
    jac, inn, variance = at_hand(jacobian, innovation, inv_variance)
    local = (table, jac, inn, counts, variance)

    coming = {"B0": across(inc)}
    if outer > 1:
        coming["A1"] = along(inc, 1)
    seen, made, gate = {"A0": inc}, {}, ()
    for kind, back in order(outer):
        name = f"{kind}{back}"
        if kind in "ABS":
            seen[name] = gate = after(coming[name], gate)
        elif kind == "z":
            source, shift = (seen[f"A{back - 1}"], 1) if back < outer - 1 else (inc, -1)
            coming[f"A{back}"] = along(after(source, gate), shift)
        elif kind == "y":
            coming[f"B{back}"] = across(after(seen[f"A{back}"], gate))
        elif kind == "w":
            coming[f"B{back}"] = along(after(seen["B0"], gate), -1)
        elif kind == "O":
            own = gate = term(padded, n, 0, False, local, inc)
        elif kind == "P":
            made[name] = gate = term(padded, n, back * inner + 1, True, local, after(seen[f"B{back}"], gate))
        elif kind == "s":
            coming[f"S{back}"] = across(after(made[f"P{back}"], gate))
        elif kind == "T":
            here = after(seen[f"A{back}"], gate)
            made[name] = gate = term(padded, n, back * inner, True, local, here, seen[f"S{back}"])
        elif kind == "r":
            coming[f"R{back}"] = along(after(made[f"T{back}"], gate), -back)
    arrived = [coming["S0"]] + [coming[f"R{back}"] for back in range(1, outer)]
    return total(own, arrived)


def solution(mesh):
    in_specs = (
        P(("member", "col"), None, None),
        P(("member", "col"), None, None),
        P(("member", "col"), None, None),
        P(),
        P(("member", "col"), None),
        P(),
        P(),
    )
    out_specs = P(("member", "col"), None, None)
    run = functools.partial(body, mesh.shape["col"])
    return jax.shard_map(run, mesh=mesh, in_specs=in_specs, out_specs=out_specs, check_vma=False)
```

time: 91.1 us -> 73.1 us (0.80)
  the two profiles are of different devices: /device:TPU:0 before, /device:TPU:16 now
where the time goes in v2:
time: 73.1 us; the launch traced here: 73.7 us
  waiting for transfers between devices  25.7 us (35%)
  Pallas kernels  22.9 us (31%)
  starting transfers between devices  21.2 us (29%)
  local copies, waits for them, and re-layouts  2.42 us (3%)
  other arithmetic  1.32 us (2%)
    ppermute x7, waiting for transfers between devices, along(): lax.ppermute(x, 'col', [(a * inner + r, b * inner + r) for a, b in lines...  25.7 us
    pallas_call x8, Pallas kernels, term(): pl.pallas_call(functools.partial(term_kernel, n, which, len(coded), packe...  17.7 us
    ppermute x7, starting transfers between devices, along(): lax.ppermute(x, 'col', [(a * inner + r, b * inner + r) for a, b in lines...  13.6 us
    ppermute x7, starting transfers between devices, across(): lax.ppermute(x, 'col', [(i, i // inner * inner + (i + 1) % inner) for i i...  7.57 us
    pallas_call x1, Pallas kernels, at_hand(): pl.pallas_call(at_hand_kernel, out_shape=(pltpu.VMEM((obs, levels, channe...  3.94 us
    unnamed x7, local copies, waits for them, and re-layouts  1.69 us
  transfers between devices with their start and end apart: 14, of which 5 were waited for; matrix products, arithmetic and copies ran while one was open for 3% of the time, Pallas kernels for 29%

profile of v2, /device:TPU:16, one launch (start us, length us, event | category | flops | bytes accessed | tf_op | source)
XLA Modules:
  0.0 73.7 jit_solution(8552085694285058868)
XLA Ops:
  0.0 0.0 copy-start
  0.0 1.0 %copy.13.inc = bf16[4,137,256]{2,1,0:T(8,128)(2,1)S(1)} copy(bf16[4,137,256]{2,0,1:T(4,128)(2,1)} %param.8) | data formatting | bytes 561152 | tf_op args[0]
  1.0 1.6 %collective-permute-start = (bf16[4,137,256]{2,1,0:T(8,128)(2,1)S(1)}, bf16[4,137,256]{2,1,0:T(8,128)(2,1)S(1)}, u32[]{:S(2)}, u32[]{:S(2)}) collective-permute-start(bf16[4,137,256]{2,1,0:T(8,128)(2,1)S(1)} %copy.13.inc), channel_id=1, source_target_pairs={{0,1},{1,0},{2,3},{3,2},{4,5},{5,4},{6,7},{7,6},{8,9},{9,8},{10,11... | collective-permute-start | bytes 841736 | tf_op jit(solution)/shard_map/ppermute | solution.py:208
  2.6 0.3 collective-permute-start.1
  2.9 0.8 %iota_add_fusion = (s32[96]{0:T(128)S(1)}, s32[96]{0:T(128)S(1)}, s32[96]{0:T(128)S(1)}) fusion(s32[768]{0:T(1024)} %param.14, s32[]{:T(128)S(6)} %select_n.11, s32[768,1]{0,1:T(1,128)} %param.13), kind=kLoop, calls=%fused_computation.7 | loop fusion | flops 576 | bytes 1924 | tf_op jit(solution)/shard_map/add | solution.py:184
  3.7 0.2 convert_reduce_fusion
  3.9 0.1 select_reduce_fusion
  4.0 0.7 dynamic-slice_bitcast_fusion
  4.7 0.0 copy-start.1
  4.7 0.7 copy-done.1
  5.4 3.9 %shard_map.82 = (bf16[96,137,128]{2,1,0:T(8,128)(2,1)S(1)}, bf16[96,128,256]{2,1,0:T(8,128)(2,1)S(1)}, f32[128,8]{1,0:T(8,128)S(1)}) custom-call(bf16[137,96,128]{2,1,0:T(8,128)(2,1)} %bitcast.9, bf16[96,128,256]{2,1,0:T(8,128)(2,1)} %inn.1, f32[1,128]{1,0:T(1,128)S(1)} %bitcast.8), custom_call_target="tpu_custom_call" | custom-call | flops 1048576 | bytes 10485760 | tf_op jit(solution)/shard_map/pallas_call | solution.py:125
  9.3 0.2 convert_reduce_fusion.2
  9.5 0.1 pad_add_fusion.table
  9.6 0.0 copy-done
  9.6 3.0 %shard_map.83.own = f32[4,137,256]{2,1,0:T(8,128)S(1)} custom-call(s32[112]{0:T(128)S(1)} %pad_add_fusion.table, bf16[4,137,256]{2,1,0:T(8,128)(2,1)S(1)} %copy.13.inc, bf16[96,137,128]{2,1,0:T(8,128)(2,1)S(1)} %get-tuple-element.28.jac, bf16[96,128,256]{2,1,0:T(8,128)(2,1)S(1)} %get-tuple-element.29.inn, s32[96,256]{1,0:T(8,128)S(1)} %copy-done, ...), custom_call_target="tpu_custom_call" | custom-call | flops 1048576 | bytes 8388608 | tf_op jit(solution)/shard_map/pallas_call | solution.py:73
  12.6 0.0 copy-start.2
  12.6 0.0 collective-permute-done.1.inc
  12.7 0.1 collective-permute-start.2
  12.7 0.3 collective-permute-start.4
  13.0 0.0 collective-permute-done.inc
  13.0 2.5 %shard_map.84 = s16[4,144,256]{2,1,0:T(8,128)(2,1)S(1)} custom-call(s32[112]{0:T(128)S(1)} %pad_add_fusion.table, bf16[4,137,256]{2,1,0:T(8,128)(2,1)S(1)} %collective-permute-done.inc, bf16[96,137,128]{2,1,0:T(8,128)(2,1)S(1)} %get-tuple-element.28.jac, bf16[96,128,256]{2,1,0:T(8,128)(2,1)S(1)} %get-tuple-element.29.inn, s32[96,256]{1,0:T(8,128)S(1)} %copy-done, ...), custom_call_target="tpu_custom_call" | custom-call | flops 1048576 | bytes 8388608 | tf_op jit(solution)/shard_map/pallas_call | solution.py:73
  15.5 5.4 %collective-permute-done.2.inc = bf16[4,137,256]{2,1,0:T(8,128)(2,1)S(1)} collective-permute-done((bf16[4,137,256]{2,1,0:T(8,128)(2,1)S(1)}, bf16[4,137,256]{2,1,0:T(8,128)(2,1)S(1)}, u32[]{:S(2)}, u32[]{:S(2)}) %collective-permute-start.2) | collective-permute-done | bytes 280608 | tf_op jit(solution)/shard_map/ppermute | solution.py:205
  20.9 0.0 collective-permute-start.3
  20.9 0.0 copy-done.2
  20.9 2.5 %collective-permute-start.8 = (bf16[4,137,256]{2,1,0:T(8,128)(2,1)S(1)}, bf16[4,137,256]{2,1,0:T(8,128)(2,1)S(1)}, u32[]{:S(2)}, u32[]{:S(2)}) collective-permute-start(bf16[4,137,256]{2,1,0:T(8,128)(2,1)S(1)} %copy.16), channel_id=1, source_target_pairs={{0,4},{1,5},{2,0},{3,1},{6,2},{7,3},{4,6},{5,7},{8,12},{9,13},{10,... | collective-permute-start | bytes 841736 | tf_op jit(solution)/shard_map/ppermute | solution.py:205
  23.5 1.8 %collective-permute-start.7 = (bf16[4,137,256]{2,1,0:T(8,128)(2,1)S(1)}, bf16[4,137,256]{2,1,0:T(8,128)(2,1)S(1)}, u32[]{:S(2)}, u32[]{:S(2)}) collective-permute-start(bf16[4,137,256]{2,1,0:T(8,128)(2,1)S(1)} %collective-permute-done.inc), channel_id=1, source_target_pairs={{0,4},{1,5},{2,0},{3,1},{6,2},{7,3},{4,6},{5,7},{8,12},{9,13},{10,... | collective-permute-start | bytes 841736 | tf_op jit(solution)/shard_map/ppermute | solution.py:205
  25.3 0.0 collective-permute-done.4.inc
  25.3 1.9 %shard_map.85 = s16[4,144,256]{2,1,0:T(8,128)(2,1)S(1)} custom-call(s32[112]{0:T(128)S(1)} %pad_add_fusion.table, bf16[4,137,256]{2,1,0:T(8,128)(2,1)S(1)} %collective-permute-done.4.inc, bf16[96,137,128]{2,1,0:T(8,128)(2,1)S(1)} %get-tuple-element.28.jac, bf16[96,128,256]{2,1,0:T(8,128)(2,1)S(1)} %get-tuple-element.29.inn, s32[96,256]{1,0:T(8,128)S(1)} %copy-done, ...), custom_call_target="tpu_custom_call" | custom-call | flops 1048576 | bytes 8388608 | tf_op jit(solution)/shard_map/pallas_call | solution.py:73
  27.2 2.1 %collective-permute-start.6 = (s16[4,144,256]{2,1,0:T(8,128)(2,1)S(1)}, s16[4,144,256]{2,1,0:T(8,128)(2,1)S(1)}, u32[]{:S(2)}, u32[]{:S(2)}) collective-permute-start(s16[4,144,256]{2,1,0:T(8,128)(2,1)S(1)} %shard_map.85), channel_id=1, source_target_pairs={{0,1},{1,0},{2,3},{3,2},{4,5},{5,4},{6,7},{7,6},{8,9},{9,8},{10,11... | collective-permute-start | bytes 884744 | tf_op jit(solution)/shard_map/ppermute | solution.py:208
  29.3 0.0 collective-permute-done.3.inc
  29.3 1.9 %shard_map.86 = s16[4,144,256]{2,1,0:T(8,128)(2,1)S(1)} custom-call(s32[112]{0:T(128)S(1)} %pad_add_fusion.table, bf16[4,137,256]{2,1,0:T(8,128)(2,1)S(1)} %collective-permute-done.3.inc, bf16[96,137,128]{2,1,0:T(8,128)(2,1)S(1)} %get-tuple-element.28.jac, bf16[96,128,256]{2,1,0:T(8,128)(2,1)S(1)} %get-tuple-element.29.inn, s32[96,256]{1,0:T(8,128)S(1)} %copy-done, ...), custom_call_target="tpu_custom_call" | custom-call | flops 1048576 | bytes 8388608 | tf_op jit(solution)/shard_map/pallas_call | solution.py:73
  31.2 0.6 collective-permute-done.8.inc
  31.8 2.0 %collective-permute-start.5 = (s16[4,144,256]{2,1,0:T(8,128)(2,1)S(1)}, s16[4,144,256]{2,1,0:T(8,128)(2,1)S(1)}, u32[]{:S(2)}, u32[]{:S(2)}) collective-permute-start(s16[4,144,256]{2,1,0:T(8,128)(2,1)S(1)} %shard_map.86), channel_id=1, source_target_pairs={{0,1},{1,0},{2,3},{3,2},{4,5},{5,4},{6,7},{7,6},{8,9},{9,8},{10,11... | collective-permute-start | bytes 884744 | tf_op jit(solution)/shard_map/ppermute | solution.py:208
  33.9 1.8 %collective-permute-done.7.inc = bf16[4,137,256]{2,1,0:T(8,128)(2,1)S(1)} collective-permute-done((bf16[4,137,256]{2,1,0:T(8,128)(2,1)S(1)}, bf16[4,137,256]{2,1,0:T(8,128)(2,1)S(1)}, u32[]{:S(2)}, u32[]{:S(2)}) %collective-permute-start.7) | collective-permute-done | bytes 280608 | tf_op jit(solution)/shard_map/ppermute | solution.py:205
  35.7 1.3 %shard_map.87 = s16[4,144,256]{2,1,0:T(8,128)(2,1)S(1)} custom-call(s32[112]{0:T(128)S(1)} %pad_add_fusion.table, bf16[4,137,256]{2,1,0:T(8,128)(2,1)S(1)} %collective-permute-done.7.inc, bf16[96,137,128]{2,1,0:T(8,128)(2,1)S(1)} %get-tuple-element.28.jac, bf16[96,128,256]{2,1,0:T(8,128)(2,1)S(1)} %get-tuple-element.29.inn, s32[96,256]{1,0:T(8,128)S(1)} %copy-done, ...), custom_call_target="tpu_custom_call" | custom-call | flops 1048576 | bytes 8388608 | tf_op jit(solution)/shard_map/pallas_call | solution.py:73
  37.0 1.6 %collective-permute-start.12 = (s16[4,144,256]{2,1,0:T(8,128)(2,1)S(1)}, s16[4,144,256]{2,1,0:T(8,128)(2,1)S(1)}, u32[]{:S(2)}, u32[]{:S(2)}) collective-permute-start(s16[4,144,256]{2,1,0:T(8,128)(2,1)S(1)} %shard_map.87), channel_id=1, source_target_pairs={{0,1},{1,0},{2,3},{3,2},{4,5},{5,4},{6,7},{7,6},{8,9},{9,8},{10,11... | collective-permute-start | bytes 884744 | tf_op jit(solution)/shard_map/ppermute | solution.py:208
  38.6 0.0 collective-permute-done.6.refs_0_
  38.6 1.9 %shard_map.88 = s16[4,144,256]{2,1,0:T(8,128)(2,1)S(1)} custom-call(s32[112]{0:T(128)S(1)} %pad_add_fusion.table, bf16[4,137,256]{2,1,0:T(8,128)(2,1)S(1)} %collective-permute-done.1.inc, bf16[96,137,128]{2,1,0:T(8,128)(2,1)S(1)} %get-tuple-element.28.jac, bf16[96,128,256]{2,1,0:T(8,128)(2,1)S(1)} %get-tuple-element.29.inn, s32[96,256]{1,0:T(8,128)S(1)} %copy-done, ...), custom_call_target="tpu_custom_call" | custom-call | flops 1048576 | bytes 8388608 | tf_op jit(solution)/shard_map/pallas_call | solution.py:73
  40.5 4.9 %collective-permute-start.10 = (s16[4,144,256]{2,1,0:T(8,128)(2,1)S(1)}, s16[4,144,256]{2,1,0:T(8,128)(2,1)S(1)}, u32[]{:S(2)}, u32[]{:S(2)}) collective-permute-start(s16[4,144,256]{2,1,0:T(8,128)(2,1)S(1)} %shard_map.88), channel_id=1, source_target_pairs={{0,4},{1,5},{2,0},{3,1},{6,2},{7,3},{4,6},{5,7},{8,12},{9,13},{10,... | collective-permute-start | bytes 884744 | tf_op jit(solution)/shard_map/ppermute | solution.py:205
  45.4 0.0 collective-permute-done.5.refs_0_
  45.4 3.1 %shard_map.89 = s16[4,144,256]{2,1,0:T(8,128)(2,1)S(1)} custom-call(s32[112]{0:T(128)S(1)} %pad_add_fusion.table, bf16[4,137,256]{2,1,0:T(8,128)(2,1)S(1)} %collective-permute-done.2.inc, bf16[96,137,128]{2,1,0:T(8,128)(2,1)S(1)} %get-tuple-element.28.jac, bf16[96,128,256]{2,1,0:T(8,128)(2,1)S(1)} %get-tuple-element.29.inn, s32[96,256]{1,0:T(8,128)S(1)} %copy-done, ...), custom_call_target="tpu_custom_call" | custom-call | flops 1048576 | bytes 8388608 | tf_op jit(solution)/shard_map/pallas_call | solution.py:73
  48.6 0.0 collective-permute-done.12.refs_0_
  48.6 1.9 %shard_map.90 = s16[4,144,256]{2,1,0:T(8,128)(2,1)S(1)} custom-call(s32[112]{0:T(128)S(1)} %pad_add_fusion.table, bf16[4,137,256]{2,1,0:T(8,128)(2,1)S(1)} %collective-permute-done.8.inc, bf16[96,137,128]{2,1,0:T(8,128)(2,1)S(1)} %get-tuple-element.28.jac, bf16[96,128,256]{2,1,0:T(8,128)(2,1)S(1)} %get-tuple-element.29.inn, s32[96,256]{1,0:T(8,128)S(1)} %copy-done, ...), custom_call_target="tpu_custom_call" | custom-call | flops 1048576 | bytes 8388608 | tf_op jit(solution)/shard_map/pallas_call | solution.py:73
  50.5 1.5 %collective-permute-start.13 = (s16[4,144,256]{2,1,0:T(8,128)(2,1)S(1)}, s16[4,144,256]{2,1,0:T(8,128)(2,1)S(1)}, u32[]{:S(2)}, u32[]{:S(2)}) collective-permute-start(s16[4,144,256]{2,1,0:T(8,128)(2,1)S(1)} %shard_map.90), channel_id=1, source_target_pairs={{0,2},{1,3},{2,6},{3,7},{6,4},{7,5},{4,0},{5,1},{8,10},{9,11},{10,... | collective-permute-start | bytes 884744 | tf_op jit(solution)/shard_map/ppermute | solution.py:205
  52.1 2.4 %collective-permute-start.11 = (s16[4,144,256]{2,1,0:T(8,128)(2,1)S(1)}, s16[4,144,256]{2,1,0:T(8,128)(2,1)S(1)}, u32[]{:S(2)}, u32[]{:S(2)}) collective-permute-start(s16[4,144,256]{2,1,0:T(8,128)(2,1)S(1)} %shard_map.89), channel_id=1, source_target_pairs={{0,6},{1,7},{2,4},{3,5},{6,0},{7,1},{4,2},{5,3},{8,14},{9,15},{10,... | collective-permute-start | bytes 884744 | tf_op jit(solution)/shard_map/ppermute | solution.py:205
  54.5 0.0 collective-permute-start.9
  54.5 0.0 collective-permute-done.10.refs_1_
  54.5 11.3 %collective-permute-done.13.refs_3_ = s16[4,144,256]{2,1,0:T(8,128)(2,1)S(1)} collective-permute-done((s16[4,144,256]{2,1,0:T(8,128)(2,1)S(1)}, s16[4,144,256]{2,1,0:T(8,128)(2,1)S(1)}, u32[]{:S(2)}, u32[]{:S(2)}) %collective-permute-start.13) | collective-permute-done | bytes 294944 | tf_op jit(solution)/shard_map/ppermute | solution.py:205
  65.8 6.6 %collective-permute-done.11.refs_2_ = s16[4,144,256]{2,1,0:T(8,128)(2,1)S(1)} collective-permute-done((s16[4,144,256]{2,1,0:T(8,128)(2,1)S(1)}, s16[4,144,256]{2,1,0:T(8,128)(2,1)S(1)}, u32[]{:S(2)}, u32[]{:S(2)}) %collective-permute-start.11) | collective-permute-done | bytes 294944 | tf_op jit(solution)/shard_map/ppermute | solution.py:205
  72.4 0.0 collective-permute-done.9.refs_0_
  72.4 1.3 %shard_map.91 = f32[137,4,256]{2,1,0:T(4,128)} custom-call(f32[4,137,256]{2,1,0:T(8,128)S(1)} %shard_map.83.own, s16[4,144,256]{2,1,0:T(8,128)(2,1)S(1)} %collective-permute-done.9.refs_0_, s16[4,144,256]{2,1,0:T(8,128)(2,1)S(1)} %collective-permute-done.10.refs_1_, s16[4,144,256]{2,1,0:T(8,128)(2,1)S(1)} %collective-permute-done.11.refs_2_, ...), custom_call_target="tpu_custom_call" | custom-call | flops 1048576 | bytes 8388608 | tf_op jit(solution)/shard_map/pallas_call | solution.py:161
  (1 shorter events, 0.0 us)
Async XLA Ops:
  0.0 9.6 %copy-start = (s32[96,256]{1,0:T(8,128)S(1)}, s32[96,256]{1,0:T(8,128)}, u32[]{:S(2)}) copy-start(s32[96,256]{1,0:T(8,128)} %cnt.15) | copy-start | bytes 294916
  1.0 12.0 %collective-permute-start = (bf16[4,137,256]{2,1,0:T(8,128)(2,1)S(1)}, bf16[4,137,256]{2,1,0:T(8,128)(2,1)S(1)}, u32[]{:S(2)}, u32[]{:S(2)}) collective-permute-start(bf16[4,137,256]{2,1,0:T(8,128)(2,1)S(1)} %copy.13.inc), channel_id=1, source_target_pairs={{0,1},{1,0},{2,3},{3,2},{4,5},{5,4},{6,7},{7,6},{8,9},{9,8},{10,11... | collective-permute-start | bytes 841736 | tf_op jit(solution)/shard_map/ppermute | solution.py:208
  2.6 10.0 %collective-permute-start.1 = (bf16[4,137,256]{2,1,0:T(8,128)(2,1)S(1)}, bf16[4,137,256]{2,1,0:T(8,128)(2,1)S(1)}, u32[]{:S(2)}, u32[]{:S(2)}) collective-permute-start(bf16[4,137,256]{2,1,0:T(8,128)(2,1)S(1)} %copy.13.inc), channel_id=1, source_target_pairs={{0,2},{1,3},{2,6},{3,7},{6,4},{7,5},{4,0},{5,1},{8,10},{9,11},{10,... | collective-permute-start | bytes 841736 | tf_op jit(solution)/shard_map/ppermute | solution.py:205
  4.7 0.7 copy-start.1
  12.6 8.3 %copy-start.2 = (bf16[4,137,256]{2,0,1:T(4,128)(2,1)S(1)}, bf16[4,137,256]{2,0,1:T(4,128)(2,1)}, u32[]{:S(2)}) copy-start(bf16[4,137,256]{2,0,1:T(4,128)(2,1)} %param.8) | copy-start | bytes 841732
  12.7 8.2 %collective-permute-start.2 = (bf16[4,137,256]{2,1,0:T(8,128)(2,1)S(1)}, bf16[4,137,256]{2,1,0:T(8,128)(2,1)S(1)}, u32[]{:S(2)}, u32[]{:S(2)}) collective-permute-start(bf16[4,137,256]{2,1,0:T(8,128)(2,1)S(1)} %collective-permute-done.1.inc), channel_id=1, source_target_pairs={{0,2},{1,3},{2,6},{3,7},{6,4},{7,5},{4,0},{5,1},{8,10},{9,11},{10,... | collective-permute-start | bytes 841736 | tf_op jit(solution)/shard_map/ppermute | solution.py:205
  12.7 12.6 %collective-permute-start.4 = (bf16[4,137,256]{2,1,0:T(8,128)(2,1)S(1)}, bf16[4,137,256]{2,1,0:T(8,128)(2,1)S(1)}, u32[]{:S(2)}, u32[]{:S(2)}) collective-permute-start(bf16[4,137,256]{2,1,0:T(8,128)(2,1)S(1)} %collective-permute-done.1.inc), channel_id=1, source_target_pairs={{0,1},{1,0},{2,3},{3,2},{4,5},{5,4},{6,7},{7,6},{8,9},{9,8},{10,11... | collective-permute-start | bytes 841736 | tf_op jit(solution)/shard_map/ppermute | solution.py:208
  20.9 8.4 %collective-permute-start.3 = (bf16[4,137,256]{2,1,0:T(8,128)(2,1)S(1)}, bf16[4,137,256]{2,1,0:T(8,128)(2,1)S(1)}, u32[]{:S(2)}, u32[]{:S(2)}) collective-permute-start(bf16[4,137,256]{2,1,0:T(8,128)(2,1)S(1)} %collective-permute-done.2.inc), channel_id=1, source_target_pairs={{0,1},{1,0},{2,3},{3,2},{4,5},{5,4},{6,7},{7,6},{8,9},{9,8},{10,11... | collective-permute-start | bytes 841736 | tf_op jit(solution)/shard_map/ppermute | solution.py:208
  20.9 10.9 %collective-permute-start.8 = (bf16[4,137,256]{2,1,0:T(8,128)(2,1)S(1)}, bf16[4,137,256]{2,1,0:T(8,128)(2,1)S(1)}, u32[]{:S(2)}, u32[]{:S(2)}) collective-permute-start(bf16[4,137,256]{2,1,0:T(8,128)(2,1)S(1)} %copy.16), channel_id=1, source_target_pairs={{0,4},{1,5},{2,0},{3,1},{6,2},{7,3},{4,6},{5,7},{8,12},{9,13},{10,... | collective-permute-start | bytes 841736 | tf_op jit(solution)/shard_map/ppermute | solution.py:205
  23.5 12.2 %collective-permute-start.7 = (bf16[4,137,256]{2,1,0:T(8,128)(2,1)S(1)}, bf16[4,137,256]{2,1,0:T(8,128)(2,1)S(1)}, u32[]{:S(2)}, u32[]{:S(2)}) collective-permute-start(bf16[4,137,256]{2,1,0:T(8,128)(2,1)S(1)} %collective-permute-done.inc), channel_id=1, source_target_pairs={{0,4},{1,5},{2,0},{3,1},{6,2},{7,3},{4,6},{5,7},{8,12},{9,13},{10,... | collective-permute-start | bytes 841736 | tf_op jit(solution)/shard_map/ppermute | solution.py:205
  27.2 11.4 %collective-permute-start.6 = (s16[4,144,256]{2,1,0:T(8,128)(2,1)S(1)}, s16[4,144,256]{2,1,0:T(8,128)(2,1)S(1)}, u32[]{:S(2)}, u32[]{:S(2)}) collective-permute-start(s16[4,144,256]{2,1,0:T(8,128)(2,1)S(1)} %shard_map.85), channel_id=1, source_target_pairs={{0,1},{1,0},{2,3},{3,2},{4,5},{5,4},{6,7},{7,6},{8,9},{9,8},{10,11... | collective-permute-start | bytes 884744 | tf_op jit(solution)/shard_map/ppermute | solution.py:208
  31.8 13.6 %collective-permute-start.5 = (s16[4,144,256]{2,1,0:T(8,128)(2,1)S(1)}, s16[4,144,256]{2,1,0:T(8,128)(2,1)S(1)}, u32[]{:S(2)}, u32[]{:S(2)}) collective-permute-start(s16[4,144,256]{2,1,0:T(8,128)(2,1)S(1)} %shard_map.86), channel_id=1, source_target_pairs={{0,1},{1,0},{2,3},{3,2},{4,5},{5,4},{6,7},{7,6},{8,9},{9,8},{10,11... | collective-permute-start | bytes 884744 | tf_op jit(solution)/shard_map/ppermute | solution.py:208
  37.0 11.6 %collective-permute-start.12 = (s16[4,144,256]{2,1,0:T(8,128)(2,1)S(1)}, s16[4,144,256]{2,1,0:T(8,128)(2,1)S(1)}, u32[]{:S(2)}, u32[]{:S(2)}) collective-permute-start(s16[4,144,256]{2,1,0:T(8,128)(2,1)S(1)} %shard_map.87), channel_id=1, source_target_pairs={{0,1},{1,0},{2,3},{3,2},{4,5},{5,4},{6,7},{7,6},{8,9},{9,8},{10,11... | collective-permute-start | bytes 884744 | tf_op jit(solution)/shard_map/ppermute | solution.py:208
  40.5 14.0 %collective-permute-start.10 = (s16[4,144,256]{2,1,0:T(8,128)(2,1)S(1)}, s16[4,144,256]{2,1,0:T(8,128)(2,1)S(1)}, u32[]{:S(2)}, u32[]{:S(2)}) collective-permute-start(s16[4,144,256]{2,1,0:T(8,128)(2,1)S(1)} %shard_map.88), channel_id=1, source_target_pairs={{0,4},{1,5},{2,0},{3,1},{6,2},{7,3},{4,6},{5,7},{8,12},{9,13},{10,... | collective-permute-start | bytes 884744 | tf_op jit(solution)/shard_map/ppermute | solution.py:205
  50.5 15.3 %collective-permute-start.13 = (s16[4,144,256]{2,1,0:T(8,128)(2,1)S(1)}, s16[4,144,256]{2,1,0:T(8,128)(2,1)S(1)}, u32[]{:S(2)}, u32[]{:S(2)}) collective-permute-start(s16[4,144,256]{2,1,0:T(8,128)(2,1)S(1)} %shard_map.90), channel_id=1, source_target_pairs={{0,2},{1,3},{2,6},{3,7},{6,4},{7,5},{4,0},{5,1},{8,10},{9,11},{10,... | collective-permute-start | bytes 884744 | tf_op jit(solution)/shard_map/ppermute | solution.py:205
  52.1 20.3 %collective-permute-start.11 = (s16[4,144,256]{2,1,0:T(8,128)(2,1)S(1)}, s16[4,144,256]{2,1,0:T(8,128)(2,1)S(1)}, u32[]{:S(2)}, u32[]{:S(2)}) collective-permute-start(s16[4,144,256]{2,1,0:T(8,128)(2,1)S(1)} %shard_map.89), channel_id=1, source_target_pairs={{0,6},{1,7},{2,4},{3,5},{6,0},{7,1},{4,2},{5,3},{8,14},{9,15},{10,... | collective-permute-start | bytes 884744 | tf_op jit(solution)/shard_map/ppermute | solution.py:205
  54.5 17.9 %collective-permute-start.9 = (s16[4,144,256]{2,1,0:T(8,128)(2,1)S(1)}, s16[4,144,256]{2,1,0:T(8,128)(2,1)S(1)}, u32[]{:S(2)}, u32[]{:S(2)}) collective-permute-start(s16[4,144,256]{2,1,0:T(8,128)(2,1)S(1)} %shard_map.84), channel_id=1, source_target_pairs={{0,1},{1,0},{2,3},{3,2},{4,5},{5,4},{6,7},{7,6},{8,9},{9,8},{10,11... | collective-permute-start | bytes 884744 | tf_op jit(solution)/shard_map/ppermute | solution.py:208

commit v3 on v2

--- a/solution.py
+++ b/solution.py
@@ -2,7 +2,6 @@
 
 import jax
 import jax.numpy as jnp
-import numpy as np
 from jax import lax
 from jax.experimental import pallas as pl
 from jax.experimental.pallas import tpu as pltpu
@@ -100,7 +99,7 @@
     return todo + [("s", 0), ("S", end), ("T", end), ("r", end)]
 
 
-def at_hand_kernel(jac, inn, iv, turned, copied, column, whole, jac_sem, inn_sem):
+def at_hand_kernel(jac, inn, iv, turned, copied, column, whole, row, jac_sem, inn_sem, row_sem):
     count = jac_sem.shape[0]
     some = jac.shape[1] // count
     copy = pltpu.make_async_copy(inn, copied, inn_sem)
@@ -110,11 +109,14 @@
     ]
     for part in parts:
         part.start()
+    lead = pltpu.make_async_copy(iv, row, row_sem)
+    lead.start()
     copy.start()
-    column[...] = jnp.swapaxes(jnp.broadcast_to(iv[...], column.shape[::-1]), 0, 1)
     for i, part in enumerate(parts):
         part.wait()
         turned[pl.ds(i * some, some)] = jnp.swapaxes(whole[:, pl.ds(i * some, some)], 0, 1)
+    lead.wait()
+    column[...] = jnp.swapaxes(jnp.broadcast_to(row[...], column.shape[::-1]), 0, 1)
     copy.wait()
 
 
@@ -129,11 +131,13 @@
             pltpu.VMEM(innovation.shape, innovation.dtype),
             pltpu.VMEM((channels, 8), inv_variance.dtype),
         ),
-        in_specs=[hbm, hbm, vmem],
+        in_specs=[hbm, hbm, hbm],
         out_specs=(vmem, vmem, vmem),
         scratch_shapes=[
             pltpu.VMEM((levels, obs, channels), jacobian.dtype),
+            pltpu.VMEM((1, channels), inv_variance.dtype),
             pltpu.SemaphoreType.DMA((obs // some,)),
+            pltpu.SemaphoreType.DMA(()),
             pltpu.SemaphoreType.DMA(()),
         ],
         compiler_params=pltpu.CompilerParams(vmem_limit_bytes=24 * 2**20),
@@ -141,7 +145,7 @@
     )(
         pltpu.with_memory_space_constraint(jnp.transpose(jacobian, (2, 0, 1)), pltpu.HBM),
         pltpu.with_memory_space_constraint(innovation, pltpu.HBM),
-        inv_variance[None, :],
+        pltpu.with_memory_space_constraint(inv_variance[None, :], pltpu.HBM),
     )
 
 
@@ -174,7 +178,7 @@
 
 
 def after(x, gate):
-    return lax.optimization_barrier((x, gate))[0]
+    return x if isinstance(gate, tuple) and not gate else lax.optimization_barrier((x, gate))[0]
 
 
 def sorted_table(owner, local_block, me, holders, obs, blocks):
@@ -208,15 +212,13 @@
         return lax.ppermute(x, "col", [(i, i // inner * inner + (i + 1) % inner) for i in range(n)])
 
     inc = increment
-    seat = {line: p for p, line in enumerate(ring)}
-    holders = np.array(
-        [
-            [ring[(seat[i // inner] - back) % outer] * inner + (i + other) % inner for back in range(outer) for other in range(inner)]
-            for i in range(n)
-        ],
-        np.int32,
-    )
-    table = sorted_table(owner, local_block, me, jnp.asarray(holders)[me], obs, blocks)
+    which = jnp.arange(n, dtype=jnp.int32)
+    line = me // inner
+    seat = jnp.where(line % 2 == 1, (line + 1) // 2, (outer - line // 2) % outer)
+    seat = (seat + outer - which // inner) % outer
+    line = jnp.where(2 * seat <= outer, jnp.maximum(2 * seat - 1, 0), 2 * (outer - seat))
+    holders = line * inner + (me + which) % inner
+    table = sorted_table(owner, local_block, me, holders, obs, blocks)
     jac, inn, variance = at_hand(jacobian, innovation, inv_variance)
     local = (table, jac, inn, counts, variance)
 

time: 73.1 us -> 71.2 us (0.974)
  the two profiles are of different devices: /device:TPU:16 before, /device:TPU:0 now
where the time goes in v3:
time: 71.2 us; the launch traced here: 69.8 us
  waiting for transfers between devices  25.8 us (36%)
  Pallas kernels  22.2 us (31%)
  starting transfers between devices  19.3 us (27%)
  other arithmetic  1.34 us (2%)
  local copies, waits for them, and re-layouts  1.02 us (1%)
    ppermute x7, waiting for transfers between devices, along(): lax.ppermute(x, 'col', [(a * inner + r, b * inner + r) for a, b in lines...  21.1 us
    pallas_call x8, Pallas kernels, term(): pl.pallas_call(functools.partial(term_kernel, n, which, len(coded), packe...  17 us
    ppermute x7, starting transfers between devices, along(): lax.ppermute(x, 'col', [(a * inner + r, b * inner + r) for a, b in lines...  13.6 us
    ppermute x7, starting transfers between devices, across(): lax.ppermute(x, 'col', [(i, i // inner * inner + (i + 1) % inner) for i i...  5.67 us
    ppermute x7, waiting for transfers between devices, across(): lax.ppermute(x, 'col', [(i, i // inner * inner + (i + 1) % inner) for i i...  4.71 us
    pallas_call x1, Pallas kernels, at_hand(): pl.pallas_call(at_hand_kernel, out_shape=(pltpu.VMEM((obs, levels, channe...  3.97 us
  transfers between devices with their start and end apart: 14, of which 5 were waited for; matrix products, arithmetic and copies ran while one was open for 2% of the time, Pallas kernels for 30%

profile of v3, /device:TPU:0, one launch (start us, length us, event | category | flops | bytes accessed | tf_op | source)
XLA Modules:
  0.0 69.8 jit_solution(16335352589469428692)
XLA Ops:
  0.0 0.0 copy-start
  0.0 1.0 %copy.12.inc = bf16[4,137,256]{2,1,0:T(8,128)(2,1)S(1)} copy(bf16[4,137,256]{2,0,1:T(4,128)(2,1)} %param.7) | data formatting | bytes 561152 | tf_op args[0]
  1.0 3.1 %collective-permute-start.1 = (bf16[4,137,256]{2,1,0:T(8,128)(2,1)S(1)}, bf16[4,137,256]{2,1,0:T(8,128)(2,1)S(1)}, u32[]{:S(2)}, u32[]{:S(2)}) collective-permute-start(bf16[4,137,256]{2,1,0:T(8,128)(2,1)S(1)} %copy.12.inc), channel_id=1, source_target_pairs={{0,2},{1,3},{2,6},{3,7},{6,4},{7,5},{4,0},{5,1},{8,10},{9,11},{10,... | collective-permute-start | bytes 841736 | tf_op jit(solution)/shard_map/ppermute | solution.py:209
  4.1 1.5 %collective-permute-start = (bf16[4,137,256]{2,1,0:T(8,128)(2,1)S(1)}, bf16[4,137,256]{2,1,0:T(8,128)(2,1)S(1)}, u32[]{:S(2)}, u32[]{:S(2)}) collective-permute-start(bf16[4,137,256]{2,1,0:T(8,128)(2,1)S(1)} %copy.12.inc), channel_id=1, source_target_pairs={{0,1},{1,0},{2,3},{3,2},{4,5},{5,4},{6,7},{7,6},{8,9},{9,8},{10,11... | collective-permute-start | bytes 841736 | tf_op jit(solution)/shard_map/ppermute | solution.py:212
  5.6 0.8 %iota_add_fusion = (s32[96]{0:T(128)S(1)}, s32[96]{0:T(128)S(1)}, s32[96]{0:T(128)S(1)}) fusion(s32[768]{0:T(1024)} %param.13, s32[]{:T(128)S(6)} %select_n.66, s32[768,1]{0,1:T(1,128)} %param.12), kind=kLoop, calls=%fused_computation.23 | loop fusion | flops 576 | bytes 1924 | tf_op jit(solution)/shard_map/add | solution.py:188
  6.4 0.2 convert_reduce_fusion
  6.6 0.1 select_reduce_fusion
  6.7 4.0 %shard_map.73 = (bf16[96,137,128]{2,1,0:T(8,128)(2,1)S(1)}, bf16[96,128,256]{2,1,0:T(8,128)(2,1)S(1)}, f32[128,8]{1,0:T(8,128)S(1)}) custom-call(bf16[137,96,128]{2,1,0:T(8,128)(2,1)} %bitcast.6, bf16[96,128,256]{2,1,0:T(8,128)(2,1)} %inn.1, f32[1,128]{1,0:T(1,128)} %bitcast.7), custom_call_target="tpu_custom_call" | custom-call | flops 1048576 | bytes 10485760 | tf_op jit(solution)/shard_map/pallas_call | solution.py:127
  10.7 0.2 convert_reduce_fusion.2
  10.9 0.1 pad_add_fusion.table
  11.0 0.0 copy-done
  11.0 3.0 %shard_map.74.own = f32[4,137,256]{2,1,0:T(8,128)S(1)} custom-call(s32[112]{0:T(128)S(1)} %pad_add_fusion.table, bf16[4,137,256]{2,1,0:T(8,128)(2,1)S(1)} %copy.12.inc, bf16[96,137,128]{2,1,0:T(8,128)(2,1)S(1)} %get-tuple-element.28.jac, bf16[96,128,256]{2,1,0:T(8,128)(2,1)S(1)} %get-tuple-element.29.inn, s32[96,256]{1,0:T(8,128)S(1)} %copy-done, ...), custom_call_target="tpu_custom_call" | custom-call | flops 1048576 | bytes 8388608 | tf_op jit(solution)/shard_map/pallas_call | solution.py:72
  14.0 0.0 collective-permute-done.1.inc
  14.0 2.0 %collective-permute-start.2 = (bf16[4,137,256]{2,1,0:T(8,128)(2,1)S(1)}, bf16[4,137,256]{2,1,0:T(8,128)(2,1)S(1)}, u32[]{:S(2)}, u32[]{:S(2)}) collective-permute-start(bf16[4,137,256]{2,1,0:T(8,128)(2,1)S(1)} %collective-permute-done.1.inc), channel_id=1, source_target_pairs={{0,2},{1,3},{2,6},{3,7},{6,4},{7,5},{4,0},{5,1},{8,10},{9,11},{10,... | collective-permute-start | bytes 841736 | tf_op jit(solution)/shard_map/ppermute | solution.py:209
  16.0 0.0 collective-permute-start.4
  16.0 0.0 collective-permute-done.inc
  16.0 1.3 %shard_map.75 = s16[4,144,256]{2,1,0:T(8,128)(2,1)S(1)} custom-call(s32[112]{0:T(128)S(1)} %pad_add_fusion.table, bf16[4,137,256]{2,1,0:T(8,128)(2,1)S(1)} %collective-permute-done.inc, bf16[96,137,128]{2,1,0:T(8,128)(2,1)S(1)} %get-tuple-element.28.jac, bf16[96,128,256]{2,1,0:T(8,128)(2,1)S(1)} %get-tuple-element.29.inn, s32[96,256]{1,0:T(8,128)S(1)} %copy-done, ...), custom_call_target="tpu_custom_call" | custom-call | flops 1048576 | bytes 8388608 | tf_op jit(solution)/shard_map/pallas_call | solution.py:72
  17.4 5.8 %collective-permute-done.2.inc = bf16[4,137,256]{2,1,0:T(8,128)(2,1)S(1)} collective-permute-done((bf16[4,137,256]{2,1,0:T(8,128)(2,1)S(1)}, bf16[4,137,256]{2,1,0:T(8,128)(2,1)S(1)}, u32[]{:S(2)}, u32[]{:S(2)}) %collective-permute-start.2) | collective-permute-done | bytes 280608 | tf_op jit(solution)/shard_map/ppermute | solution.py:209
  23.1 0.0 collective-permute-start.3
  23.1 0.9 %collective-permute-start.8 = (bf16[4,137,256]{2,1,0:T(8,128)(2,1)S(1)}, bf16[4,137,256]{2,1,0:T(8,128)(2,1)S(1)}, u32[]{:S(2)}, u32[]{:S(2)}) collective-permute-start(bf16[4,137,256]{2,1,0:T(8,128)(2,1)S(1)} %copy.12.inc), channel_id=1, source_target_pairs={{0,4},{1,5},{2,0},{3,1},{6,2},{7,3},{4,6},{5,7},{8,12},{9,13},{10,... | collective-permute-start | bytes 841736 | tf_op jit(solution)/shard_map/ppermute | solution.py:209
  24.0 2.6 %collective-permute-start.7 = (bf16[4,137,256]{2,1,0:T(8,128)(2,1)S(1)}, bf16[4,137,256]{2,1,0:T(8,128)(2,1)S(1)}, u32[]{:S(2)}, u32[]{:S(2)}) collective-permute-start(bf16[4,137,256]{2,1,0:T(8,128)(2,1)S(1)} %collective-permute-done.inc), channel_id=1, source_target_pairs={{0,4},{1,5},{2,0},{3,1},{6,2},{7,3},{4,6},{5,7},{8,12},{9,13},{10,... | collective-permute-start | bytes 841736 | tf_op jit(solution)/shard_map/ppermute | solution.py:209
  26.6 0.0 collective-permute-done.4.inc
  26.6 1.9 %shard_map.76 = s16[4,144,256]{2,1,0:T(8,128)(2,1)S(1)} custom-call(s32[112]{0:T(128)S(1)} %pad_add_fusion.table, bf16[4,137,256]{2,1,0:T(8,128)(2,1)S(1)} %collective-permute-done.4.inc, bf16[96,137,128]{2,1,0:T(8,128)(2,1)S(1)} %get-tuple-element.28.jac, bf16[96,128,256]{2,1,0:T(8,128)(2,1)S(1)} %get-tuple-element.29.inn, s32[96,256]{1,0:T(8,128)S(1)} %copy-done, ...), custom_call_target="tpu_custom_call" | custom-call | flops 1048576 | bytes 8388608 | tf_op jit(solution)/shard_map/pallas_call | solution.py:72
  28.5 1.5 %collective-permute-start.6 = (s16[4,144,256]{2,1,0:T(8,128)(2,1)S(1)}, s16[4,144,256]{2,1,0:T(8,128)(2,1)S(1)}, u32[]{:S(2)}, u32[]{:S(2)}) collective-permute-start(s16[4,144,256]{2,1,0:T(8,128)(2,1)S(1)} %shard_map.76), channel_id=1, source_target_pairs={{0,1},{1,0},{2,3},{3,2},{4,5},{5,4},{6,7},{7,6},{8,9},{9,8},{10,11... | collective-permute-start | bytes 884744 | tf_op jit(solution)/shard_map/ppermute | solution.py:212
  30.0 2.3 %collective-permute-done.3.inc = bf16[4,137,256]{2,1,0:T(8,128)(2,1)S(1)} collective-permute-done((bf16[4,137,256]{2,1,0:T(8,128)(2,1)S(1)}, bf16[4,137,256]{2,1,0:T(8,128)(2,1)S(1)}, u32[]{:S(2)}, u32[]{:S(2)}) %collective-permute-start.3) | collective-permute-done | bytes 280608 | tf_op jit(solution)/shard_map/ppermute | solution.py:212
  32.3 2.5 %shard_map.77 = s16[4,144,256]{2,1,0:T(8,128)(2,1)S(1)} custom-call(s32[112]{0:T(128)S(1)} %pad_add_fusion.table, bf16[4,137,256]{2,1,0:T(8,128)(2,1)S(1)} %collective-permute-done.3.inc, bf16[96,137,128]{2,1,0:T(8,128)(2,1)S(1)} %get-tuple-element.28.jac, bf16[96,128,256]{2,1,0:T(8,128)(2,1)S(1)} %get-tuple-element.29.inn, s32[96,256]{1,0:T(8,128)S(1)} %copy-done, ...), custom_call_target="tpu_custom_call" | custom-call | flops 1048576 | bytes 8388608 | tf_op jit(solution)/shard_map/pallas_call | solution.py:72
  34.8 0.0 collective-permute-done.8.inc
  34.8 0.3 collective-permute-start.5
  35.1 1.6 %collective-permute-done.7.inc = bf16[4,137,256]{2,1,0:T(8,128)(2,1)S(1)} collective-permute-done((bf16[4,137,256]{2,1,0:T(8,128)(2,1)S(1)}, bf16[4,137,256]{2,1,0:T(8,128)(2,1)S(1)}, u32[]{:S(2)}, u32[]{:S(2)}) %collective-permute-start.7) | collective-permute-done | bytes 280608 | tf_op jit(solution)/shard_map/ppermute | solution.py:209
  36.7 1.3 %shard_map.78 = s16[4,144,256]{2,1,0:T(8,128)(2,1)S(1)} custom-call(s32[112]{0:T(128)S(1)} %pad_add_fusion.table, bf16[4,137,256]{2,1,0:T(8,128)(2,1)S(1)} %collective-permute-done.7.inc, bf16[96,137,128]{2,1,0:T(8,128)(2,1)S(1)} %get-tuple-element.28.jac, bf16[96,128,256]{2,1,0:T(8,128)(2,1)S(1)} %get-tuple-element.29.inn, s32[96,256]{1,0:T(8,128)S(1)} %copy-done, ...), custom_call_target="tpu_custom_call" | custom-call | flops 1048576 | bytes 8388608 | tf_op jit(solution)/shard_map/pallas_call | solution.py:72
  38.0 2.4 %collective-permute-start.12 = (s16[4,144,256]{2,1,0:T(8,128)(2,1)S(1)}, s16[4,144,256]{2,1,0:T(8,128)(2,1)S(1)}, u32[]{:S(2)}, u32[]{:S(2)}) collective-permute-start(s16[4,144,256]{2,1,0:T(8,128)(2,1)S(1)} %shard_map.78), channel_id=1, source_target_pairs={{0,1},{1,0},{2,3},{3,2},{4,5},{5,4},{6,7},{7,6},{8,9},{9,8},{10,11... | collective-permute-start | bytes 884744 | tf_op jit(solution)/shard_map/ppermute | solution.py:212
  40.4 0.0 collective-permute-done.6.refs_0_
  40.4 3.1 %shard_map.79 = s16[4,144,256]{2,1,0:T(8,128)(2,1)S(1)} custom-call(s32[112]{0:T(128)S(1)} %pad_add_fusion.table, bf16[4,137,256]{2,1,0:T(8,128)(2,1)S(1)} %collective-permute-done.1.inc, bf16[96,137,128]{2,1,0:T(8,128)(2,1)S(1)} %get-tuple-element.28.jac, bf16[96,128,256]{2,1,0:T(8,128)(2,1)S(1)} %get-tuple-element.29.inn, s32[96,256]{1,0:T(8,128)S(1)} %copy-done, ...), custom_call_target="tpu_custom_call" | custom-call | flops 1048576 | bytes 8388608 | tf_op jit(solution)/shard_map/pallas_call | solution.py:72
  43.6 1.4 %collective-permute-start.10 = (s16[4,144,256]{2,1,0:T(8,128)(2,1)S(1)}, s16[4,144,256]{2,1,0:T(8,128)(2,1)S(1)}, u32[]{:S(2)}, u32[]{:S(2)}) collective-permute-start(s16[4,144,256]{2,1,0:T(8,128)(2,1)S(1)} %shard_map.79), channel_id=1, source_target_pairs={{0,4},{1,5},{2,0},{3,1},{6,2},{7,3},{4,6},{5,7},{8,12},{9,13},{10,... | collective-permute-start | bytes 884744 | tf_op jit(solution)/shard_map/ppermute | solution.py:209
  45.0 0.0 collective-permute-done.5.refs_0_
  45.0 1.9 %shard_map.80 = s16[4,144,256]{2,1,0:T(8,128)(2,1)S(1)} custom-call(s32[112]{0:T(128)S(1)} %pad_add_fusion.table, bf16[4,137,256]{2,1,0:T(8,128)(2,1)S(1)} %collective-permute-done.2.inc, bf16[96,137,128]{2,1,0:T(8,128)(2,1)S(1)} %get-tuple-element.28.jac, bf16[96,128,256]{2,1,0:T(8,128)(2,1)S(1)} %get-tuple-element.29.inn, s32[96,256]{1,0:T(8,128)S(1)} %copy-done, ...), custom_call_target="tpu_custom_call" | custom-call | flops 1048576 | bytes 8388608 | tf_op jit(solution)/shard_map/pallas_call | solution.py:72
  47.0 2.4 %collective-permute-done.12.refs_0_ = s16[4,144,256]{2,1,0:T(8,128)(2,1)S(1)} collective-permute-done((s16[4,144,256]{2,1,0:T(8,128)(2,1)S(1)}, s16[4,144,256]{2,1,0:T(8,128)(2,1)S(1)}, u32[]{:S(2)}, u32[]{:S(2)}) %collective-permute-start.12) | collective-permute-done | bytes 294944 | tf_op jit(solution)/shard_map/ppermute | solution.py:212
  49.4 1.9 %shard_map.81 = s16[4,144,256]{2,1,0:T(8,128)(2,1)S(1)} custom-call(s32[112]{0:T(128)S(1)} %pad_add_fusion.table, bf16[4,137,256]{2,1,0:T(8,128)(2,1)S(1)} %collective-permute-done.8.inc, bf16[96,137,128]{2,1,0:T(8,128)(2,1)S(1)} %get-tuple-element.28.jac, bf16[96,128,256]{2,1,0:T(8,128)(2,1)S(1)} %get-tuple-element.29.inn, s32[96,256]{1,0:T(8,128)S(1)} %copy-done, ...), custom_call_target="tpu_custom_call" | custom-call | flops 1048576 | bytes 8388608 | tf_op jit(solution)/shard_map/pallas_call | solution.py:72
  51.3 1.1 %collective-permute-start.13 = (s16[4,144,256]{2,1,0:T(8,128)(2,1)S(1)}, s16[4,144,256]{2,1,0:T(8,128)(2,1)S(1)}, u32[]{:S(2)}, u32[]{:S(2)}) collective-permute-start(s16[4,144,256]{2,1,0:T(8,128)(2,1)S(1)} %shard_map.81), channel_id=1, source_target_pairs={{0,2},{1,3},{2,6},{3,7},{6,4},{7,5},{4,0},{5,1},{8,10},{9,11},{10,... | collective-permute-start | bytes 884744 | tf_op jit(solution)/shard_map/ppermute | solution.py:209
  52.4 2.4 %collective-permute-start.11 = (s16[4,144,256]{2,1,0:T(8,128)(2,1)S(1)}, s16[4,144,256]{2,1,0:T(8,128)(2,1)S(1)}, u32[]{:S(2)}, u32[]{:S(2)}) collective-permute-start(s16[4,144,256]{2,1,0:T(8,128)(2,1)S(1)} %shard_map.80), channel_id=1, source_target_pairs={{0,6},{1,7},{2,4},{3,5},{6,0},{7,1},{4,2},{5,3},{8,14},{9,15},{10,... | collective-permute-start | bytes 884744 | tf_op jit(solution)/shard_map/ppermute | solution.py:209
  54.8 0.0 collective-permute-start.9
  54.8 0.0 collective-permute-done.10.refs_1_
  54.8 13.7 %collective-permute-done.13.refs_3_ = s16[4,144,256]{2,1,0:T(8,128)(2,1)S(1)} collective-permute-done((s16[4,144,256]{2,1,0:T(8,128)(2,1)S(1)}, s16[4,144,256]{2,1,0:T(8,128)(2,1)S(1)}, u32[]{:S(2)}, u32[]{:S(2)}) %collective-permute-start.13) | collective-permute-done | bytes 294944 | tf_op jit(solution)/shard_map/ppermute | solution.py:209
  68.5 0.0 collective-permute-done.11.refs_2_
  68.5 0.0 collective-permute-done.9.refs_0_
  68.5 1.3 %shard_map.82 = f32[137,4,256]{2,1,0:T(4,128)} custom-call(f32[4,137,256]{2,1,0:T(8,128)S(1)} %shard_map.74.own, s16[4,144,256]{2,1,0:T(8,128)(2,1)S(1)} %collective-permute-done.9.refs_0_, s16[4,144,256]{2,1,0:T(8,128)(2,1)S(1)} %collective-permute-done.10.refs_1_, s16[4,144,256]{2,1,0:T(8,128)(2,1)S(1)} %collective-permute-done.11.refs_2_, ...), custom_call_target="tpu_custom_call" | custom-call | flops 1048576 | bytes 8388608 | tf_op jit(solution)/shard_map/pallas_call | solution.py:165
  (1 shorter events, 0.0 us)
Async XLA Ops:
  0.0 11.0 %copy-start = (s32[96,256]{1,0:T(8,128)S(1)}, s32[96,256]{1,0:T(8,128)}, u32[]{:S(2)}) copy-start(s32[96,256]{1,0:T(8,128)} %cnt.15) | copy-start | bytes 294916
  1.0 13.0 %collective-permute-start.1 = (bf16[4,137,256]{2,1,0:T(8,128)(2,1)S(1)}, bf16[4,137,256]{2,1,0:T(8,128)(2,1)S(1)}, u32[]{:S(2)}, u32[]{:S(2)}) collective-permute-start(bf16[4,137,256]{2,1,0:T(8,128)(2,1)S(1)} %copy.12.inc), channel_id=1, source_target_pairs={{0,2},{1,3},{2,6},{3,7},{6,4},{7,5},{4,0},{5,1},{8,10},{9,11},{10,... | collective-permute-start | bytes 841736 | tf_op jit(solution)/shard_map/ppermute | solution.py:209
  4.1 11.9 %collective-permute-start = (bf16[4,137,256]{2,1,0:T(8,128)(2,1)S(1)}, bf16[4,137,256]{2,1,0:T(8,128)(2,1)S(1)}, u32[]{:S(2)}, u32[]{:S(2)}) collective-permute-start(bf16[4,137,256]{2,1,0:T(8,128)(2,1)S(1)} %copy.12.inc), channel_id=1, source_target_pairs={{0,1},{1,0},{2,3},{3,2},{4,5},{5,4},{6,7},{7,6},{8,9},{9,8},{10,11... | collective-permute-start | bytes 841736 | tf_op jit(solution)/shard_map/ppermute | solution.py:212
  14.0 9.1 %collective-permute-start.2 = (bf16[4,137,256]{2,1,0:T(8,128)(2,1)S(1)}, bf16[4,137,256]{2,1,0:T(8,128)(2,1)S(1)}, u32[]{:S(2)}, u32[]{:S(2)}) collective-permute-start(bf16[4,137,256]{2,1,0:T(8,128)(2,1)S(1)} %collective-permute-done.1.inc), channel_id=1, source_target_pairs={{0,2},{1,3},{2,6},{3,7},{6,4},{7,5},{4,0},{5,1},{8,10},{9,11},{10,... | collective-permute-start | bytes 841736 | tf_op jit(solution)/shard_map/ppermute | solution.py:209
  16.0 10.6 %collective-permute-start.4 = (bf16[4,137,256]{2,1,0:T(8,128)(2,1)S(1)}, bf16[4,137,256]{2,1,0:T(8,128)(2,1)S(1)}, u32[]{:S(2)}, u32[]{:S(2)}) collective-permute-start(bf16[4,137,256]{2,1,0:T(8,128)(2,1)S(1)} %collective-permute-done.1.inc), channel_id=1, source_target_pairs={{0,1},{1,0},{2,3},{3,2},{4,5},{5,4},{6,7},{7,6},{8,9},{9,8},{10,11... | collective-permute-start | bytes 841736 | tf_op jit(solution)/shard_map/ppermute | solution.py:212
  23.1 9.2 %collective-permute-start.3 = (bf16[4,137,256]{2,1,0:T(8,128)(2,1)S(1)}, bf16[4,137,256]{2,1,0:T(8,128)(2,1)S(1)}, u32[]{:S(2)}, u32[]{:S(2)}) collective-permute-start(bf16[4,137,256]{2,1,0:T(8,128)(2,1)S(1)} %collective-permute-done.2.inc), channel_id=1, source_target_pairs={{0,1},{1,0},{2,3},{3,2},{4,5},{5,4},{6,7},{7,6},{8,9},{9,8},{10,11... | collective-permute-start | bytes 841736 | tf_op jit(solution)/shard_map/ppermute | solution.py:212
  23.1 11.7 %collective-permute-start.8 = (bf16[4,137,256]{2,1,0:T(8,128)(2,1)S(1)}, bf16[4,137,256]{2,1,0:T(8,128)(2,1)S(1)}, u32[]{:S(2)}, u32[]{:S(2)}) collective-permute-start(bf16[4,137,256]{2,1,0:T(8,128)(2,1)S(1)} %copy.12.inc), channel_id=1, source_target_pairs={{0,4},{1,5},{2,0},{3,1},{6,2},{7,3},{4,6},{5,7},{8,12},{9,13},{10,... | collective-permute-start | bytes 841736 | tf_op jit(solution)/shard_map/ppermute | solution.py:209
  24.0 12.7 %collective-permute-start.7 = (bf16[4,137,256]{2,1,0:T(8,128)(2,1)S(1)}, bf16[4,137,256]{2,1,0:T(8,128)(2,1)S(1)}, u32[]{:S(2)}, u32[]{:S(2)}) collective-permute-start(bf16[4,137,256]{2,1,0:T(8,128)(2,1)S(1)} %collective-permute-done.inc), channel_id=1, source_target_pairs={{0,4},{1,5},{2,0},{3,1},{6,2},{7,3},{4,6},{5,7},{8,12},{9,13},{10,... | collective-permute-start | bytes 841736 | tf_op jit(solution)/shard_map/ppermute | solution.py:209
  28.5 11.9 %collective-permute-start.6 = (s16[4,144,256]{2,1,0:T(8,128)(2,1)S(1)}, s16[4,144,256]{2,1,0:T(8,128)(2,1)S(1)}, u32[]{:S(2)}, u32[]{:S(2)}) collective-permute-start(s16[4,144,256]{2,1,0:T(8,128)(2,1)S(1)} %shard_map.76), channel_id=1, source_target_pairs={{0,1},{1,0},{2,3},{3,2},{4,5},{5,4},{6,7},{7,6},{8,9},{9,8},{10,11... | collective-permute-start | bytes 884744 | tf_op jit(solution)/shard_map/ppermute | solution.py:212
  34.8 10.2 %collective-permute-start.5 = (s16[4,144,256]{2,1,0:T(8,128)(2,1)S(1)}, s16[4,144,256]{2,1,0:T(8,128)(2,1)S(1)}, u32[]{:S(2)}, u32[]{:S(2)}) collective-permute-start(s16[4,144,256]{2,1,0:T(8,128)(2,1)S(1)} %shard_map.77), channel_id=1, source_target_pairs={{0,1},{1,0},{2,3},{3,2},{4,5},{5,4},{6,7},{7,6},{8,9},{9,8},{10,11... | collective-permute-start | bytes 884744 | tf_op jit(solution)/shard_map/ppermute | solution.py:212
  38.0 11.3 %collective-permute-start.12 = (s16[4,144,256]{2,1,0:T(8,128)(2,1)S(1)}, s16[4,144,256]{2,1,0:T(8,128)(2,1)S(1)}, u32[]{:S(2)}, u32[]{:S(2)}) collective-permute-start(s16[4,144,256]{2,1,0:T(8,128)(2,1)S(1)} %shard_map.78), channel_id=1, source_target_pairs={{0,1},{1,0},{2,3},{3,2},{4,5},{5,4},{6,7},{7,6},{8,9},{9,8},{10,11... | collective-permute-start | bytes 884744 | tf_op jit(solution)/shard_map/ppermute | solution.py:212
  43.6 11.2 %collective-permute-start.10 = (s16[4,144,256]{2,1,0:T(8,128)(2,1)S(1)}, s16[4,144,256]{2,1,0:T(8,128)(2,1)S(1)}, u32[]{:S(2)}, u32[]{:S(2)}) collective-permute-start(s16[4,144,256]{2,1,0:T(8,128)(2,1)S(1)} %shard_map.79), channel_id=1, source_target_pairs={{0,4},{1,5},{2,0},{3,1},{6,2},{7,3},{4,6},{5,7},{8,12},{9,13},{10,... | collective-permute-start | bytes 884744 | tf_op jit(solution)/shard_map/ppermute | solution.py:209
  51.3 17.2 %collective-permute-start.13 = (s16[4,144,256]{2,1,0:T(8,128)(2,1)S(1)}, s16[4,144,256]{2,1,0:T(8,128)(2,1)S(1)}, u32[]{:S(2)}, u32[]{:S(2)}) collective-permute-start(s16[4,144,256]{2,1,0:T(8,128)(2,1)S(1)} %shard_map.81), channel_id=1, source_target_pairs={{0,2},{1,3},{2,6},{3,7},{6,4},{7,5},{4,0},{5,1},{8,10},{9,11},{10,... | collective-permute-start | bytes 884744 | tf_op jit(solution)/shard_map/ppermute | solution.py:209
  52.4 16.1 %collective-permute-start.11 = (s16[4,144,256]{2,1,0:T(8,128)(2,1)S(1)}, s16[4,144,256]{2,1,0:T(8,128)(2,1)S(1)}, u32[]{:S(2)}, u32[]{:S(2)}) collective-permute-start(s16[4,144,256]{2,1,0:T(8,128)(2,1)S(1)} %shard_map.80), channel_id=1, source_target_pairs={{0,6},{1,7},{2,4},{3,5},{6,0},{7,1},{4,2},{5,3},{8,14},{9,15},{10,... | collective-permute-start | bytes 884744 | tf_op jit(solution)/shard_map/ppermute | solution.py:209
  54.8 13.7 %collective-permute-start.9 = (s16[4,144,256]{2,1,0:T(8,128)(2,1)S(1)}, s16[4,144,256]{2,1,0:T(8,128)(2,1)S(1)}, u32[]{:S(2)}, u32[]{:S(2)}) collective-permute-start(s16[4,144,256]{2,1,0:T(8,128)(2,1)S(1)} %shard_map.75), channel_id=1, source_target_pairs={{0,1},{1,0},{2,3},{3,2},{4,5},{5,4},{6,7},{7,6},{8,9},{9,8},{10,11... | collective-permute-start | bytes 884744 | tf_op jit(solution)/shard_map/ppermute | solution.py:212

commit v4 on v3

--- a/solution.py
+++ b/solution.py
@@ -87,10 +87,10 @@
         todo += [(kind, 0) for kind in "OBPs"]
         todo += [(kind, k) for k in range(1, outer) for kind in "BPs"]
         return todo + [(kind, k) for k in range(1, outer) for kind in "STr"]
-    todo = [("z", end), ("A", 1), ("O", 0), ("z", 2), ("y", 1), ("B", 0), ("w", end), ("P", 0)]
+    todo = [("z", end), ("L", 0), ("A", 1), ("z", 2), ("y", 1), ("B", 0), ("P", 0)]
     for k in range(2, end):
         todo += [("A", k), ("z", k + 1), ("y", k)] if k + 1 < end else [("A", k), ("y", k)]
-        todo += [(kind, k - 1) for kind in "BPs"]
+        todo += [("B", k - 1), ("P", k - 1)] + [("w", end)] * (k == 2) + [("s", k - 1)] + [("O", 0)] * (k == 2)
         if k > 3:
             todo += [(kind, k - 3) for kind in "STr"]
     todo += [(kind, end - 1) for kind in "BPs"]
@@ -237,6 +237,8 @@
             coming[f"B{back}"] = across(after(seen[f"A{back}"], gate))
         elif kind == "w":
             coming[f"B{back}"] = along(after(seen["B0"], gate), -1)
+        elif kind == "L":
+            gate = (jac, inn)
         elif kind == "O":
             own = gate = term(padded, n, 0, False, local, inc)
         elif kind == "P":
@@ -248,7 +250,7 @@
             made[name] = gate = term(padded, n, back * inner, True, local, here, seen[f"S{back}"])
         elif kind == "r":
             coming[f"R{back}"] = along(after(made[f"T{back}"], gate), -back)
-    arrived = [coming["S0"]] + [coming[f"R{back}"] for back in range(1, outer)]
+    arrived = [coming[name] for name in coming if name[0] == "R" or name == "S0"]
     return total(own, arrived)
 
 

time: 71.2 us -> 70.2 us (0.986); the launches traced: 69.8 us -> 70.3 us
    ppermute x7, waiting for transfers between devices: 21.1 us -> 24.7 us  [along(): lax.ppermute(x, 'col', [(a * inner + r, b * inner + r) for a, b in lines...]
    ppermute x7, waiting for transfers between devices: 4.71 us -> 1.44 us  [across(): lax.ppermute(x, 'col', [(i, i // inner * inner + (i + 1) % inner) for i i...]
    ppermute x7, starting transfers between devices: 5.67 us -> 6.72 us  [across(): lax.ppermute(x, 'col', [(i, i // inner * inner + (i + 1) % inner) for i i...]
    ppermute x7, starting transfers between devices: 13.6 us -> 12.7 us  [along(): lax.ppermute(x, 'col', [(a * inner + r, b * inner + r) for a, b in lines...]
  transfers between devices with their start and end apart: 14 -> 14, of which waited for: 5 -> 7; matrix products, arithmetic and copies ran while one was open for 2% -> 2% of each run, Pallas kernels for 30% -> 30%
where the time goes in v4:
time: 70.2 us; the launch traced here: 70.3 us
  waiting for transfers between devices  26.2 us (37%)
  Pallas kernels  22.2 us (32%)
  starting transfers between devices  19.4 us (28%)
  other arithmetic  1.34 us (2%)
  local copies, waits for them, and re-layouts  1.02 us (1%)
    ppermute x7, waiting for transfers between devices, along(): lax.ppermute(x, 'col', [(a * inner + r, b * inner + r) for a, b in lines...  24.7 us
    pallas_call x8, Pallas kernels, term(): pl.pallas_call(functools.partial(term_kernel, n, which, len(coded), packe...  17 us
    ppermute x7, starting transfers between devices, along(): lax.ppermute(x, 'col', [(a * inner + r, b * inner + r) for a, b in lines...  12.7 us
    ppermute x7, starting transfers between devices, across(): lax.ppermute(x, 'col', [(i, i // inner * inner + (i + 1) % inner) for i i...  6.72 us
    pallas_call x1, Pallas kernels, at_hand(): pl.pallas_call(at_hand_kernel, out_shape=(pltpu.VMEM((obs, levels, channe...  3.97 us
    ppermute x7, waiting for transfers between devices, across(): lax.ppermute(x, 'col', [(i, i // inner * inner + (i + 1) % inner) for i i...  1.44 us
  transfers between devices with their start and end apart: 14, of which 7 were waited for; matrix products, arithmetic and copies ran while one was open for 2% of the time, Pallas kernels for 30%

profile of v4, /device:TPU:0, one launch (start us, length us, event | category | flops | bytes accessed | tf_op | source)
XLA Modules:
  0.0 70.3 jit_solution(382315731003564668)
XLA Ops:
  0.0 0.0 copy-start
  0.0 1.0 %copy.12.inc = bf16[4,137,256]{2,1,0:T(8,128)(2,1)S(1)} copy(bf16[4,137,256]{2,0,1:T(4,128)(2,1)} %param.7) | data formatting | bytes 561152 | tf_op args[0]
  1.0 3.0 %collective-permute-start.3 = (bf16[4,137,256]{2,1,0:T(8,128)(2,1)S(1)}, bf16[4,137,256]{2,1,0:T(8,128)(2,1)S(1)}, u32[]{:S(2)}, u32[]{:S(2)}) collective-permute-start(bf16[4,137,256]{2,1,0:T(8,128)(2,1)S(1)} %copy.12.inc), channel_id=1, source_target_pairs={{0,1},{1,0},{2,3},{3,2},{4,5},{5,4},{6,7},{7,6},{8,9},{9,8},{10,11... | collective-permute-start | bytes 841736 | tf_op jit(solution)/shard_map/ppermute | solution.py:212
  4.1 1.6 %collective-permute-start = (bf16[4,137,256]{2,1,0:T(8,128)(2,1)S(1)}, bf16[4,137,256]{2,1,0:T(8,128)(2,1)S(1)}, u32[]{:S(2)}, u32[]{:S(2)}) collective-permute-start(bf16[4,137,256]{2,1,0:T(8,128)(2,1)S(1)} %copy.12.inc), channel_id=1, source_target_pairs={{0,2},{1,3},{2,6},{3,7},{6,4},{7,5},{4,0},{5,1},{8,10},{9,11},{10,... | collective-permute-start | bytes 841736 | tf_op jit(solution)/shard_map/ppermute | solution.py:209
  5.6 0.8 %iota_add_fusion = (s32[96]{0:T(128)S(1)}, s32[96]{0:T(128)S(1)}, s32[96]{0:T(128)S(1)}) fusion(s32[768]{0:T(1024)} %param.13, s32[]{:T(128)S(6)} %select_n.66, s32[768,1]{0,1:T(1,128)} %param.12), kind=kLoop, calls=%fused_computation.23 | loop fusion | flops 576 | bytes 1924 | tf_op jit(solution)/shard_map/add | solution.py:188
  6.4 4.0 %shard_map.73 = (bf16[96,137,128]{2,1,0:T(8,128)(2,1)S(1)}, bf16[96,128,256]{2,1,0:T(8,128)(2,1)S(1)}, f32[128,8]{1,0:T(8,128)S(1)}) custom-call(bf16[137,96,128]{2,1,0:T(8,128)(2,1)} %bitcast.6, bf16[96,128,256]{2,1,0:T(8,128)(2,1)} %inn.1, f32[1,128]{1,0:T(1,128)} %bitcast.7), custom_call_target="tpu_custom_call" | custom-call | flops 1048576 | bytes 10485760 | tf_op jit(solution)/shard_map/pallas_call | solution.py:127
  10.4 0.2 convert_reduce_fusion
  10.6 0.1 select_reduce_fusion
  10.7 2.7 %collective-permute-done.inc = bf16[4,137,256]{2,1,0:T(8,128)(2,1)S(1)} collective-permute-done((bf16[4,137,256]{2,1,0:T(8,128)(2,1)S(1)}, bf16[4,137,256]{2,1,0:T(8,128)(2,1)S(1)}, u32[]{:S(2)}, u32[]{:S(2)}) %collective-permute-start) | collective-permute-done | bytes 280608 | tf_op jit(solution)/shard_map/ppermute | solution.py:209
  13.4 0.8 %collective-permute-start.2 = (bf16[4,137,256]{2,1,0:T(8,128)(2,1)S(1)}, bf16[4,137,256]{2,1,0:T(8,128)(2,1)S(1)}, u32[]{:S(2)}, u32[]{:S(2)}) collective-permute-start(bf16[4,137,256]{2,1,0:T(8,128)(2,1)S(1)} %collective-permute-done.inc), channel_id=1, source_target_pairs={{0,2},{1,3},{2,6},{3,7},{6,4},{7,5},{4,0},{5,1},{8,10},{9,11},{10,... | collective-permute-start | bytes 841736 | tf_op jit(solution)/shard_map/ppermute | solution.py:209
  14.2 0.5 collective-permute-start.1
  14.7 0.2 convert_reduce_fusion.2
  14.9 0.1 pad_add_fusion.table
  15.0 0.0 collective-permute-done.3.inc
  15.0 0.0 copy-done
  15.0 1.9 %shard_map.75 = s16[4,144,256]{2,1,0:T(8,128)(2,1)S(1)} custom-call(s32[112]{0:T(128)S(1)} %pad_add_fusion.table, bf16[4,137,256]{2,1,0:T(8,128)(2,1)S(1)} %collective-permute-done.3.inc, bf16[96,137,128]{2,1,0:T(8,128)(2,1)S(1)} %get-tuple-element.31.jac, bf16[96,128,256]{2,1,0:T(8,128)(2,1)S(1)} %get-tuple-element.32.inn, s32[96,256]{1,0:T(8,128)S(1)} %copy-done, ...), custom_call_target="tpu_custom_call" | custom-call | flops 1048576 | bytes 8388608 | tf_op jit(solution)/shard_map/pallas_call | solution.py:72
  16.9 5.0 %collective-permute-done.2.inc = bf16[4,137,256]{2,1,0:T(8,128)(2,1)S(1)} collective-permute-done((bf16[4,137,256]{2,1,0:T(8,128)(2,1)S(1)}, bf16[4,137,256]{2,1,0:T(8,128)(2,1)S(1)}, u32[]{:S(2)}, u32[]{:S(2)}) %collective-permute-start.2) | collective-permute-done | bytes 280608 | tf_op jit(solution)/shard_map/ppermute | solution.py:209
  21.9 0.8 %collective-permute-start.7 = (bf16[4,137,256]{2,1,0:T(8,128)(2,1)S(1)}, bf16[4,137,256]{2,1,0:T(8,128)(2,1)S(1)}, u32[]{:S(2)}, u32[]{:S(2)}) collective-permute-start(bf16[4,137,256]{2,1,0:T(8,128)(2,1)S(1)} %collective-permute-done.2.inc), channel_id=1, source_target_pairs={{0,1},{1,0},{2,3},{3,2},{4,5},{5,4},{6,7},{7,6},{8,9},{9,8},{10,11... | collective-permute-start | bytes 841736 | tf_op jit(solution)/shard_map/ppermute | solution.py:212
  22.7 1.3 %collective-permute-start.6 = (bf16[4,137,256]{2,1,0:T(8,128)(2,1)S(1)}, bf16[4,137,256]{2,1,0:T(8,128)(2,1)S(1)}, u32[]{:S(2)}, u32[]{:S(2)}) collective-permute-start(bf16[4,137,256]{2,1,0:T(8,128)(2,1)S(1)} %copy.12.inc), channel_id=1, source_target_pairs={{0,4},{1,5},{2,0},{3,1},{6,2},{7,3},{4,6},{5,7},{8,12},{9,13},{10,... | collective-permute-start | bytes 841736 | tf_op jit(solution)/shard_map/ppermute | solution.py:209
  23.9 0.0 collective-permute-done.1.inc
  23.9 3.1 %shard_map.76 = s16[4,144,256]{2,1,0:T(8,128)(2,1)S(1)} custom-call(s32[112]{0:T(128)S(1)} %pad_add_fusion.table, bf16[4,137,256]{2,1,0:T(8,128)(2,1)S(1)} %collective-permute-done.1.inc, bf16[96,137,128]{2,1,0:T(8,128)(2,1)S(1)} %get-tuple-element.31.jac, bf16[96,128,256]{2,1,0:T(8,128)(2,1)S(1)} %get-tuple-element.32.inn, s32[96,256]{1,0:T(8,128)S(1)} %copy-done, ...), custom_call_target="tpu_custom_call" | custom-call | flops 1048576 | bytes 8388608 | tf_op jit(solution)/shard_map/pallas_call | solution.py:72
  27.0 1.5 %collective-permute-start.5 = (bf16[4,137,256]{2,1,0:T(8,128)(2,1)S(1)}, bf16[4,137,256]{2,1,0:T(8,128)(2,1)S(1)}, u32[]{:S(2)}, u32[]{:S(2)}) collective-permute-start(bf16[4,137,256]{2,1,0:T(8,128)(2,1)S(1)} %collective-permute-done.3.inc), channel_id=1, source_target_pairs={{0,4},{1,5},{2,0},{3,1},{6,2},{7,3},{4,6},{5,7},{8,12},{9,13},{10,... | collective-permute-start | bytes 841736 | tf_op jit(solution)/shard_map/ppermute | solution.py:209
  28.5 1.5 %collective-permute-start.4 = (s16[4,144,256]{2,1,0:T(8,128)(2,1)S(1)}, s16[4,144,256]{2,1,0:T(8,128)(2,1)S(1)}, u32[]{:S(2)}, u32[]{:S(2)}) collective-permute-start(s16[4,144,256]{2,1,0:T(8,128)(2,1)S(1)} %shard_map.76), channel_id=1, source_target_pairs={{0,1},{1,0},{2,3},{3,2},{4,5},{5,4},{6,7},{7,6},{8,9},{9,8},{10,11... | collective-permute-start | bytes 884744 | tf_op jit(solution)/shard_map/ppermute | solution.py:212
  30.0 1.2 %shard_map.74.own = f32[4,137,256]{2,1,0:T(8,128)S(1)} custom-call(s32[112]{0:T(128)S(1)} %pad_add_fusion.table, bf16[4,137,256]{2,1,0:T(8,128)(2,1)S(1)} %copy.12.inc, bf16[96,137,128]{2,1,0:T(8,128)(2,1)S(1)} %get-tuple-element.31.jac, bf16[96,128,256]{2,1,0:T(8,128)(2,1)S(1)} %get-tuple-element.32.inn, s32[96,256]{1,0:T(8,128)S(1)} %copy-done, ...), custom_call_target="tpu_custom_call" | custom-call | flops 1048576 | bytes 8388608 | tf_op jit(solution)/shard_map/pallas_call | solution.py:72
  31.3 0.0 collective-permute-done.7.inc
  31.3 1.9 %shard_map.77 = s16[4,144,256]{2,1,0:T(8,128)(2,1)S(1)} custom-call(s32[112]{0:T(128)S(1)} %pad_add_fusion.table, bf16[4,137,256]{2,1,0:T(8,128)(2,1)S(1)} %collective-permute-done.7.inc, bf16[96,137,128]{2,1,0:T(8,128)(2,1)S(1)} %get-tuple-element.31.jac, bf16[96,128,256]{2,1,0:T(8,128)(2,1)S(1)} %get-tuple-element.32.inn, s32[96,256]{1,0:T(8,128)S(1)} %copy-done, ...), custom_call_target="tpu_custom_call" | custom-call | flops 1048576 | bytes 8388608 | tf_op jit(solution)/shard_map/pallas_call | solution.py:72
  33.2 0.1 collective-permute-start.9
  33.3 0.0 collective-permute-done.6.inc
  33.3 2.4 %collective-permute-done.5.inc = bf16[4,137,256]{2,1,0:T(8,128)(2,1)S(1)} collective-permute-done((bf16[4,137,256]{2,1,0:T(8,128)(2,1)S(1)}, bf16[4,137,256]{2,1,0:T(8,128)(2,1)S(1)}, u32[]{:S(2)}, u32[]{:S(2)}) %collective-permute-start.5) | collective-permute-done | bytes 280608 | tf_op jit(solution)/shard_map/ppermute | solution.py:209
  35.7 2.5 %shard_map.78 = s16[4,144,256]{2,1,0:T(8,128)(2,1)S(1)} custom-call(s32[112]{0:T(128)S(1)} %pad_add_fusion.table, bf16[4,137,256]{2,1,0:T(8,128)(2,1)S(1)} %collective-permute-done.5.inc, bf16[96,137,128]{2,1,0:T(8,128)(2,1)S(1)} %get-tuple-element.31.jac, bf16[96,128,256]{2,1,0:T(8,128)(2,1)S(1)} %get-tuple-element.32.inn, s32[96,256]{1,0:T(8,128)S(1)} %copy-done, ...), custom_call_target="tpu_custom_call" | custom-call | flops 1048576 | bytes 8388608 | tf_op jit(solution)/shard_map/pallas_call | solution.py:72
  38.2 0.7 %collective-permute-start.12 = (s16[4,144,256]{2,1,0:T(8,128)(2,1)S(1)}, s16[4,144,256]{2,1,0:T(8,128)(2,1)S(1)}, u32[]{:S(2)}, u32[]{:S(2)}) collective-permute-start(s16[4,144,256]{2,1,0:T(8,128)(2,1)S(1)} %shard_map.78), channel_id=1, source_target_pairs={{0,1},{1,0},{2,3},{3,2},{4,5},{5,4},{6,7},{7,6},{8,9},{9,8},{10,11... | collective-permute-start | bytes 884744 | tf_op jit(solution)/shard_map/ppermute | solution.py:212
  38.9 0.0 collective-permute-done.4.refs_0_
  38.9 3.1 %shard_map.79 = s16[4,144,256]{2,1,0:T(8,128)(2,1)S(1)} custom-call(s32[112]{0:T(128)S(1)} %pad_add_fusion.table, bf16[4,137,256]{2,1,0:T(8,128)(2,1)S(1)} %collective-permute-done.inc, bf16[96,137,128]{2,1,0:T(8,128)(2,1)S(1)} %get-tuple-element.31.jac, bf16[96,128,256]{2,1,0:T(8,128)(2,1)S(1)} %get-tuple-element.32.inn, s32[96,256]{1,0:T(8,128)S(1)} %copy-done, ...), custom_call_target="tpu_custom_call" | custom-call | flops 1048576 | bytes 8388608 | tf_op jit(solution)/shard_map/pallas_call | solution.py:72
  42.1 1.3 %collective-permute-start.8 = (s16[4,144,256]{2,1,0:T(8,128)(2,1)S(1)}, s16[4,144,256]{2,1,0:T(8,128)(2,1)S(1)}, u32[]{:S(2)}, u32[]{:S(2)}) collective-permute-start(s16[4,144,256]{2,1,0:T(8,128)(2,1)S(1)} %shard_map.79), channel_id=1, source_target_pairs={{0,4},{1,5},{2,0},{3,1},{6,2},{7,3},{4,6},{5,7},{8,12},{9,13},{10,... | collective-permute-start | bytes 884744 | tf_op jit(solution)/shard_map/ppermute | solution.py:209
  43.3 1.0 %collective-permute-done.9.refs_0_ = s16[4,144,256]{2,1,0:T(8,128)(2,1)S(1)} collective-permute-done((s16[4,144,256]{2,1,0:T(8,128)(2,1)S(1)}, s16[4,144,256]{2,1,0:T(8,128)(2,1)S(1)}, u32[]{:S(2)}, u32[]{:S(2)}) %collective-permute-start.9) | collective-permute-done | bytes 294944 | tf_op jit(solution)/shard_map/ppermute | solution.py:212
  44.4 1.9 %shard_map.80 = s16[4,144,256]{2,1,0:T(8,128)(2,1)S(1)} custom-call(s32[112]{0:T(128)S(1)} %pad_add_fusion.table, bf16[4,137,256]{2,1,0:T(8,128)(2,1)S(1)} %collective-permute-done.2.inc, bf16[96,137,128]{2,1,0:T(8,128)(2,1)S(1)} %get-tuple-element.31.jac, bf16[96,128,256]{2,1,0:T(8,128)(2,1)S(1)} %get-tuple-element.32.inn, s32[96,256]{1,0:T(8,128)S(1)} %copy-done, ...), custom_call_target="tpu_custom_call" | custom-call | flops 1048576 | bytes 8388608 | tf_op jit(solution)/shard_map/pallas_call | solution.py:72
  46.3 3.0 %collective-permute-start.10 = (s16[4,144,256]{2,1,0:T(8,128)(2,1)S(1)}, s16[4,144,256]{2,1,0:T(8,128)(2,1)S(1)}, u32[]{:S(2)}, u32[]{:S(2)}) collective-permute-start(s16[4,144,256]{2,1,0:T(8,128)(2,1)S(1)} %shard_map.80), channel_id=1, source_target_pairs={{0,6},{1,7},{2,4},{3,5},{6,0},{7,1},{4,2},{5,3},{8,14},{9,15},{10,... | collective-permute-start | bytes 884744 | tf_op jit(solution)/shard_map/ppermute | solution.py:209
  49.3 0.1 collective-permute-start.11
  49.4 0.4 collective-permute-done.12.refs_0_
  49.8 1.3 %shard_map.81 = s16[4,144,256]{2,1,0:T(8,128)(2,1)S(1)} custom-call(s32[112]{0:T(128)S(1)} %pad_add_fusion.table, bf16[4,137,256]{2,1,0:T(8,128)(2,1)S(1)} %collective-permute-done.6.inc, bf16[96,137,128]{2,1,0:T(8,128)(2,1)S(1)} %get-tuple-element.31.jac, bf16[96,128,256]{2,1,0:T(8,128)(2,1)S(1)} %get-tuple-element.32.inn, s32[96,256]{1,0:T(8,128)S(1)} %copy-done, ...), custom_call_target="tpu_custom_call" | custom-call | flops 1048576 | bytes 8388608 | tf_op jit(solution)/shard_map/pallas_call | solution.py:72
  51.1 3.3 %collective-permute-start.13 = (s16[4,144,256]{2,1,0:T(8,128)(2,1)S(1)}, s16[4,144,256]{2,1,0:T(8,128)(2,1)S(1)}, u32[]{:S(2)}, u32[]{:S(2)}) collective-permute-start(s16[4,144,256]{2,1,0:T(8,128)(2,1)S(1)} %shard_map.81), channel_id=1, source_target_pairs={{0,2},{1,3},{2,6},{3,7},{6,4},{7,5},{4,0},{5,1},{8,10},{9,11},{10,... | collective-permute-start | bytes 884744 | tf_op jit(solution)/shard_map/ppermute | solution.py:209
  54.4 0.0 collective-permute-done.8.refs_0_
  54.4 5.2 %collective-permute-done.10.refs_1_ = s16[4,144,256]{2,1,0:T(8,128)(2,1)S(1)} collective-permute-done((s16[4,144,256]{2,1,0:T(8,128)(2,1)S(1)}, s16[4,144,256]{2,1,0:T(8,128)(2,1)S(1)}, u32[]{:S(2)}, u32[]{:S(2)}) %collective-permute-start.10) | collective-permute-done | bytes 294944 | tf_op jit(solution)/shard_map/ppermute | solution.py:209
  59.6 0.0 collective-permute-done.11.refs_2_
  59.6 9.4 %collective-permute-done.13.refs_3_ = s16[4,144,256]{2,1,0:T(8,128)(2,1)S(1)} collective-permute-done((s16[4,144,256]{2,1,0:T(8,128)(2,1)S(1)}, s16[4,144,256]{2,1,0:T(8,128)(2,1)S(1)}, u32[]{:S(2)}, u32[]{:S(2)}) %collective-permute-start.13) | collective-permute-done | bytes 294944 | tf_op jit(solution)/shard_map/ppermute | solution.py:209
  69.0 1.3 %shard_map.82 = f32[137,4,256]{2,1,0:T(4,128)} custom-call(f32[4,137,256]{2,1,0:T(8,128)S(1)} %shard_map.74.own, s16[4,144,256]{2,1,0:T(8,128)(2,1)S(1)} %collective-permute-done.8.refs_0_, s16[4,144,256]{2,1,0:T(8,128)(2,1)S(1)} %collective-permute-done.10.refs_1_, s16[4,144,256]{2,1,0:T(8,128)(2,1)S(1)} %collective-permute-done.11.refs_2_, ...), custom_call_target="tpu_custom_call" | custom-call | flops 1048576 | bytes 8388608 | tf_op jit(solution)/shard_map/pallas_call | solution.py:165
  (1 shorter events, 0.0 us)
Async XLA Ops:
  0.0 15.0 %copy-start = (s32[96,256]{1,0:T(8,128)S(1)}, s32[96,256]{1,0:T(8,128)}, u32[]{:S(2)}) copy-start(s32[96,256]{1,0:T(8,128)} %cnt.15) | copy-start | bytes 294916
  1.0 14.0 %collective-permute-start.3 = (bf16[4,137,256]{2,1,0:T(8,128)(2,1)S(1)}, bf16[4,137,256]{2,1,0:T(8,128)(2,1)S(1)}, u32[]{:S(2)}, u32[]{:S(2)}) collective-permute-start(bf16[4,137,256]{2,1,0:T(8,128)(2,1)S(1)} %copy.12.inc), channel_id=1, source_target_pairs={{0,1},{1,0},{2,3},{3,2},{4,5},{5,4},{6,7},{7,6},{8,9},{9,8},{10,11... | collective-permute-start | bytes 841736 | tf_op jit(solution)/shard_map/ppermute | solution.py:212
  4.1 9.4 %collective-permute-start = (bf16[4,137,256]{2,1,0:T(8,128)(2,1)S(1)}, bf16[4,137,256]{2,1,0:T(8,128)(2,1)S(1)}, u32[]{:S(2)}, u32[]{:S(2)}) collective-permute-start(bf16[4,137,256]{2,1,0:T(8,128)(2,1)S(1)} %copy.12.inc), channel_id=1, source_target_pairs={{0,2},{1,3},{2,6},{3,7},{6,4},{7,5},{4,0},{5,1},{8,10},{9,11},{10,... | collective-permute-start | bytes 841736 | tf_op jit(solution)/shard_map/ppermute | solution.py:209
  13.4 8.5 %collective-permute-start.2 = (bf16[4,137,256]{2,1,0:T(8,128)(2,1)S(1)}, bf16[4,137,256]{2,1,0:T(8,128)(2,1)S(1)}, u32[]{:S(2)}, u32[]{:S(2)}) collective-permute-start(bf16[4,137,256]{2,1,0:T(8,128)(2,1)S(1)} %collective-permute-done.inc), channel_id=1, source_target_pairs={{0,2},{1,3},{2,6},{3,7},{6,4},{7,5},{4,0},{5,1},{8,10},{9,11},{10,... | collective-permute-start | bytes 841736 | tf_op jit(solution)/shard_map/ppermute | solution.py:209
  14.2 9.7 %collective-permute-start.1 = (bf16[4,137,256]{2,1,0:T(8,128)(2,1)S(1)}, bf16[4,137,256]{2,1,0:T(8,128)(2,1)S(1)}, u32[]{:S(2)}, u32[]{:S(2)}) collective-permute-start(bf16[4,137,256]{2,1,0:T(8,128)(2,1)S(1)} %collective-permute-done.inc), channel_id=1, source_target_pairs={{0,1},{1,0},{2,3},{3,2},{4,5},{5,4},{6,7},{7,6},{8,9},{9,8},{10,11... | collective-permute-start | bytes 841736 | tf_op jit(solution)/shard_map/ppermute | solution.py:212
  21.9 9.4 %collective-permute-start.7 = (bf16[4,137,256]{2,1,0:T(8,128)(2,1)S(1)}, bf16[4,137,256]{2,1,0:T(8,128)(2,1)S(1)}, u32[]{:S(2)}, u32[]{:S(2)}) collective-permute-start(bf16[4,137,256]{2,1,0:T(8,128)(2,1)S(1)} %collective-permute-done.2.inc), channel_id=1, source_target_pairs={{0,1},{1,0},{2,3},{3,2},{4,5},{5,4},{6,7},{7,6},{8,9},{9,8},{10,11... | collective-permute-start | bytes 841736 | tf_op jit(solution)/shard_map/ppermute | solution.py:212
  22.7 10.6 %collective-permute-start.6 = (bf16[4,137,256]{2,1,0:T(8,128)(2,1)S(1)}, bf16[4,137,256]{2,1,0:T(8,128)(2,1)S(1)}, u32[]{:S(2)}, u32[]{:S(2)}) collective-permute-start(bf16[4,137,256]{2,1,0:T(8,128)(2,1)S(1)} %copy.12.inc), channel_id=1, source_target_pairs={{0,4},{1,5},{2,0},{3,1},{6,2},{7,3},{4,6},{5,7},{8,12},{9,13},{10,... | collective-permute-start | bytes 841736 | tf_op jit(solution)/shard_map/ppermute | solution.py:209
  27.0 8.7 %collective-permute-start.5 = (bf16[4,137,256]{2,1,0:T(8,128)(2,1)S(1)}, bf16[4,137,256]{2,1,0:T(8,128)(2,1)S(1)}, u32[]{:S(2)}, u32[]{:S(2)}) collective-permute-start(bf16[4,137,256]{2,1,0:T(8,128)(2,1)S(1)} %collective-permute-done.3.inc), channel_id=1, source_target_pairs={{0,4},{1,5},{2,0},{3,1},{6,2},{7,3},{4,6},{5,7},{8,12},{9,13},{10,... | collective-permute-start | bytes 841736 | tf_op jit(solution)/shard_map/ppermute | solution.py:209
  28.5 10.4 %collective-permute-start.4 = (s16[4,144,256]{2,1,0:T(8,128)(2,1)S(1)}, s16[4,144,256]{2,1,0:T(8,128)(2,1)S(1)}, u32[]{:S(2)}, u32[]{:S(2)}) collective-permute-start(s16[4,144,256]{2,1,0:T(8,128)(2,1)S(1)} %shard_map.76), channel_id=1, source_target_pairs={{0,1},{1,0},{2,3},{3,2},{4,5},{5,4},{6,7},{7,6},{8,9},{9,8},{10,11... | collective-permute-start | bytes 884744 | tf_op jit(solution)/shard_map/ppermute | solution.py:212
  33.2 11.2 %collective-permute-start.9 = (s16[4,144,256]{2,1,0:T(8,128)(2,1)S(1)}, s16[4,144,256]{2,1,0:T(8,128)(2,1)S(1)}, u32[]{:S(2)}, u32[]{:S(2)}) collective-permute-start(s16[4,144,256]{2,1,0:T(8,128)(2,1)S(1)} %shard_map.77), channel_id=1, source_target_pairs={{0,1},{1,0},{2,3},{3,2},{4,5},{5,4},{6,7},{7,6},{8,9},{9,8},{10,11... | collective-permute-start | bytes 884744 | tf_op jit(solution)/shard_map/ppermute | solution.py:212
  38.2 11.6 %collective-permute-start.12 = (s16[4,144,256]{2,1,0:T(8,128)(2,1)S(1)}, s16[4,144,256]{2,1,0:T(8,128)(2,1)S(1)}, u32[]{:S(2)}, u32[]{:S(2)}) collective-permute-start(s16[4,144,256]{2,1,0:T(8,128)(2,1)S(1)} %shard_map.78), channel_id=1, source_target_pairs={{0,1},{1,0},{2,3},{3,2},{4,5},{5,4},{6,7},{7,6},{8,9},{9,8},{10,11... | collective-permute-start | bytes 884744 | tf_op jit(solution)/shard_map/ppermute | solution.py:212
  42.1 12.4 %collective-permute-start.8 = (s16[4,144,256]{2,1,0:T(8,128)(2,1)S(1)}, s16[4,144,256]{2,1,0:T(8,128)(2,1)S(1)}, u32[]{:S(2)}, u32[]{:S(2)}) collective-permute-start(s16[4,144,256]{2,1,0:T(8,128)(2,1)S(1)} %shard_map.79), channel_id=1, source_target_pairs={{0,4},{1,5},{2,0},{3,1},{6,2},{7,3},{4,6},{5,7},{8,12},{9,13},{10,... | collective-permute-start | bytes 884744 | tf_op jit(solution)/shard_map/ppermute | solution.py:209
  46.3 13.3 %collective-permute-start.10 = (s16[4,144,256]{2,1,0:T(8,128)(2,1)S(1)}, s16[4,144,256]{2,1,0:T(8,128)(2,1)S(1)}, u32[]{:S(2)}, u32[]{:S(2)}) collective-permute-start(s16[4,144,256]{2,1,0:T(8,128)(2,1)S(1)} %shard_map.80), channel_id=1, source_target_pairs={{0,6},{1,7},{2,4},{3,5},{6,0},{7,1},{4,2},{5,3},{8,14},{9,15},{10,... | collective-permute-start | bytes 884744 | tf_op jit(solution)/shard_map/ppermute | solution.py:209
  49.3 10.3 %collective-permute-start.11 = (s16[4,144,256]{2,1,0:T(8,128)(2,1)S(1)}, s16[4,144,256]{2,1,0:T(8,128)(2,1)S(1)}, u32[]{:S(2)}, u32[]{:S(2)}) collective-permute-start(s16[4,144,256]{2,1,0:T(8,128)(2,1)S(1)} %shard_map.75), channel_id=1, source_target_pairs={{0,1},{1,0},{2,3},{3,2},{4,5},{5,4},{6,7},{7,6},{8,9},{9,8},{10,11... | collective-permute-start | bytes 884744 | tf_op jit(solution)/shard_map/ppermute | solution.py:212
  51.1 17.9 %collective-permute-start.13 = (s16[4,144,256]{2,1,0:T(8,128)(2,1)S(1)}, s16[4,144,256]{2,1,0:T(8,128)(2,1)S(1)}, u32[]{:S(2)}, u32[]{:S(2)}) collective-permute-start(s16[4,144,256]{2,1,0:T(8,128)(2,1)S(1)} %shard_map.81), channel_id=1, source_target_pairs={{0,2},{1,3},{2,6},{3,7},{6,4},{7,5},{4,0},{5,1},{8,10},{9,11},{10,... | collective-permute-start | bytes 884744 | tf_op jit(solution)/shard_map/ppermute | solution.py:209

commit v5 on v4

--- a/solution.py
+++ b/solution.py
@@ -87,10 +87,10 @@
         todo += [(kind, 0) for kind in "OBPs"]
         todo += [(kind, k) for k in range(1, outer) for kind in "BPs"]
         return todo + [(kind, k) for k in range(1, outer) for kind in "STr"]
-    todo = [("z", end), ("L", 0), ("A", 1), ("z", 2), ("y", 1), ("B", 0), ("P", 0)]
+    todo = [("z", end), ("L", 0), ("A", 1), ("z", 2), ("y", 1), ("O", 0), ("B", 0)]
     for k in range(2, end):
         todo += [("A", k), ("z", k + 1), ("y", k)] if k + 1 < end else [("A", k), ("y", k)]
-        todo += [("B", k - 1), ("P", k - 1)] + [("w", end)] * (k == 2) + [("s", k - 1)] + [("O", 0)] * (k == 2)
+        todo += [("B", k - 1), ("P", k - 1)] + [("w", end)] * (k == 2) + [("s", k - 1)] + [("P", 0)] * (k == 2)
         if k > 3:
             todo += [(kind, k - 3) for kind in "STr"]
     todo += [(kind, end - 1) for kind in "BPs"]

time: 70.2 us -> 69.9 us (level); the launches traced: 70.3 us -> 69.2 us
  Pallas kernels: 22.2 us -> 21 us
    ppermute x7, waiting for transfers between devices: 1.44 us -> 3.78 us  [across(): lax.ppermute(x, 'col', [(i, i // inner * inner + (i + 1) % inner) for i i...]
    ppermute x7, waiting for transfers between devices: 24.7 us -> 22.4 us  [along(): lax.ppermute(x, 'col', [(a * inner + r, b * inner + r) for a, b in lines...]
    ppermute x7, starting transfers between devices: 6.72 us -> 8.09 us  [across(): lax.ppermute(x, 'col', [(i, i // inner * inner + (i + 1) % inner) for i i...]
    ppermute x7, starting transfers between devices: 12.7 us -> 11.4 us  [along(): lax.ppermute(x, 'col', [(a * inner + r, b * inner + r) for a, b in lines...]
    pallas_call x8, Pallas kernels: 17 us -> 15.8 us  [term(): pl.pallas_call(functools.partial(term_kernel, n, which, len(coded), packe...]
  transfers between devices with their start and end apart: 14 -> 14, of which waited for: 7 -> 5; matrix products, arithmetic and copies ran while one was open for 2% -> 2% of each run, Pallas kernels for 30% -> 29%
where the time goes in v5:
time: 69.9 us; the launch traced here: 69.2 us
  waiting for transfers between devices  26.2 us (37%)
  Pallas kernels  21 us (30%)
  starting transfers between devices  19.5 us (28%)
  other arithmetic  1.34 us (2%)
  local copies, waits for them, and re-layouts  1.02 us (1%)
    ppermute x7, waiting for transfers between devices, along(): lax.ppermute(x, 'col', [(a * inner + r, b * inner + r) for a, b in lines...  22.4 us
    pallas_call x8, Pallas kernels, term(): pl.pallas_call(functools.partial(term_kernel, n, which, len(coded), packe...  15.8 us
    ppermute x7, starting transfers between devices, along(): lax.ppermute(x, 'col', [(a * inner + r, b * inner + r) for a, b in lines...  11.4 us
    ppermute x7, starting transfers between devices, across(): lax.ppermute(x, 'col', [(i, i // inner * inner + (i + 1) % inner) for i i...  8.09 us
    pallas_call x1, Pallas kernels, at_hand(): pl.pallas_call(at_hand_kernel, out_shape=(pltpu.VMEM((obs, levels, channe...  3.97 us
    ppermute x7, waiting for transfers between devices, across(): lax.ppermute(x, 'col', [(i, i // inner * inner + (i + 1) % inner) for i i...  3.78 us
  transfers between devices with their start and end apart: 14, of which 5 were waited for; matrix products, arithmetic and copies ran while one was open for 2% of the time, Pallas kernels for 29%

profile of v5, /device:TPU:0, one launch (start us, length us, event | category | flops | bytes accessed | tf_op | source)
XLA Modules:
  0.0 69.2 jit_solution(8140022768835196515)
XLA Ops:
  0.0 0.0 copy-start
  0.0 1.0 %copy.12.inc = bf16[4,137,256]{2,1,0:T(8,128)(2,1)S(1)} copy(bf16[4,137,256]{2,0,1:T(4,128)(2,1)} %param.7) | data formatting | bytes 561152 | tf_op args[0]
  1.0 3.0 %collective-permute-start.3 = (bf16[4,137,256]{2,1,0:T(8,128)(2,1)S(1)}, bf16[4,137,256]{2,1,0:T(8,128)(2,1)S(1)}, u32[]{:S(2)}, u32[]{:S(2)}) collective-permute-start(bf16[4,137,256]{2,1,0:T(8,128)(2,1)S(1)} %copy.12.inc), channel_id=1, source_target_pairs={{0,1},{1,0},{2,3},{3,2},{4,5},{5,4},{6,7},{7,6},{8,9},{9,8},{10,11... | collective-permute-start | bytes 841736 | tf_op jit(solution)/shard_map/ppermute | solution.py:212
  4.1 1.6 %collective-permute-start = (bf16[4,137,256]{2,1,0:T(8,128)(2,1)S(1)}, bf16[4,137,256]{2,1,0:T(8,128)(2,1)S(1)}, u32[]{:S(2)}, u32[]{:S(2)}) collective-permute-start(bf16[4,137,256]{2,1,0:T(8,128)(2,1)S(1)} %copy.12.inc), channel_id=1, source_target_pairs={{0,2},{1,3},{2,6},{3,7},{6,4},{7,5},{4,0},{5,1},{8,10},{9,11},{10,... | collective-permute-start | bytes 841736 | tf_op jit(solution)/shard_map/ppermute | solution.py:209
  5.6 0.8 %iota_add_fusion = (s32[96]{0:T(128)S(1)}, s32[96]{0:T(128)S(1)}, s32[96]{0:T(128)S(1)}) fusion(s32[768]{0:T(1024)} %param.13, s32[]{:T(128)S(6)} %select_n.66, s32[768,1]{0,1:T(1,128)} %param.12), kind=kLoop, calls=%fused_computation.23 | loop fusion | flops 576 | bytes 1924 | tf_op jit(solution)/shard_map/add | solution.py:188
  6.4 4.0 %shard_map.73 = (bf16[96,137,128]{2,1,0:T(8,128)(2,1)S(1)}, bf16[96,128,256]{2,1,0:T(8,128)(2,1)S(1)}, f32[128,8]{1,0:T(8,128)S(1)}) custom-call(bf16[137,96,128]{2,1,0:T(8,128)(2,1)} %bitcast.6, bf16[96,128,256]{2,1,0:T(8,128)(2,1)} %inn.1, f32[1,128]{1,0:T(1,128)} %bitcast.7), custom_call_target="tpu_custom_call" | custom-call | flops 1048576 | bytes 10485760 | tf_op jit(solution)/shard_map/pallas_call | solution.py:127
  10.4 0.2 convert_reduce_fusion
  10.6 0.1 select_reduce_fusion
  10.7 2.7 %collective-permute-done.inc = bf16[4,137,256]{2,1,0:T(8,128)(2,1)S(1)} collective-permute-done((bf16[4,137,256]{2,1,0:T(8,128)(2,1)S(1)}, bf16[4,137,256]{2,1,0:T(8,128)(2,1)S(1)}, u32[]{:S(2)}, u32[]{:S(2)}) %collective-permute-start) | collective-permute-done | bytes 280608 | tf_op jit(solution)/shard_map/ppermute | solution.py:209
  13.4 0.8 %collective-permute-start.2 = (bf16[4,137,256]{2,1,0:T(8,128)(2,1)S(1)}, bf16[4,137,256]{2,1,0:T(8,128)(2,1)S(1)}, u32[]{:S(2)}, u32[]{:S(2)}) collective-permute-start(bf16[4,137,256]{2,1,0:T(8,128)(2,1)S(1)} %collective-permute-done.inc), channel_id=1, source_target_pairs={{0,2},{1,3},{2,6},{3,7},{6,4},{7,5},{4,0},{5,1},{8,10},{9,11},{10,... | collective-permute-start | bytes 841736 | tf_op jit(solution)/shard_map/ppermute | solution.py:209
  14.2 0.5 collective-permute-start.1
  14.7 0.2 convert_reduce_fusion.2
  14.9 0.1 pad_add_fusion.table
  15.0 0.0 copy-done
  15.0 1.2 %shard_map.74.own = f32[4,137,256]{2,1,0:T(8,128)S(1)} custom-call(s32[112]{0:T(128)S(1)} %pad_add_fusion.table, bf16[4,137,256]{2,1,0:T(8,128)(2,1)S(1)} %copy.12.inc, bf16[96,137,128]{2,1,0:T(8,128)(2,1)S(1)} %get-tuple-element.30.jac, bf16[96,128,256]{2,1,0:T(8,128)(2,1)S(1)} %get-tuple-element.31.inn, s32[96,256]{1,0:T(8,128)S(1)} %copy-done, ...), custom_call_target="tpu_custom_call" | custom-call | flops 1048576 | bytes 8388608 | tf_op jit(solution)/shard_map/pallas_call | solution.py:72
  16.2 0.0 collective-permute-done.3.inc
  16.2 5.6 %collective-permute-done.2.inc = bf16[4,137,256]{2,1,0:T(8,128)(2,1)S(1)} collective-permute-done((bf16[4,137,256]{2,1,0:T(8,128)(2,1)S(1)}, bf16[4,137,256]{2,1,0:T(8,128)(2,1)S(1)}, u32[]{:S(2)}, u32[]{:S(2)}) %collective-permute-start.2) | collective-permute-done | bytes 280608 | tf_op jit(solution)/shard_map/ppermute | solution.py:209
  21.9 0.8 %collective-permute-start.7 = (bf16[4,137,256]{2,1,0:T(8,128)(2,1)S(1)}, bf16[4,137,256]{2,1,0:T(8,128)(2,1)S(1)}, u32[]{:S(2)}, u32[]{:S(2)}) collective-permute-start(bf16[4,137,256]{2,1,0:T(8,128)(2,1)S(1)} %collective-permute-done.2.inc), channel_id=1, source_target_pairs={{0,1},{1,0},{2,3},{3,2},{4,5},{5,4},{6,7},{7,6},{8,9},{9,8},{10,11... | collective-permute-start | bytes 841736 | tf_op jit(solution)/shard_map/ppermute | solution.py:212
  22.7 1.3 %collective-permute-start.6 = (bf16[4,137,256]{2,1,0:T(8,128)(2,1)S(1)}, bf16[4,137,256]{2,1,0:T(8,128)(2,1)S(1)}, u32[]{:S(2)}, u32[]{:S(2)}) collective-permute-start(bf16[4,137,256]{2,1,0:T(8,128)(2,1)S(1)} %copy.12.inc), channel_id=1, source_target_pairs={{0,4},{1,5},{2,0},{3,1},{6,2},{7,3},{4,6},{5,7},{8,12},{9,13},{10,... | collective-permute-start | bytes 841736 | tf_op jit(solution)/shard_map/ppermute | solution.py:209
  23.9 0.0 collective-permute-done.1.inc
  23.9 1.9 %shard_map.75 = s16[4,144,256]{2,1,0:T(8,128)(2,1)S(1)} custom-call(s32[112]{0:T(128)S(1)} %pad_add_fusion.table, bf16[4,137,256]{2,1,0:T(8,128)(2,1)S(1)} %collective-permute-done.1.inc, bf16[96,137,128]{2,1,0:T(8,128)(2,1)S(1)} %get-tuple-element.30.jac, bf16[96,128,256]{2,1,0:T(8,128)(2,1)S(1)} %get-tuple-element.31.inn, s32[96,256]{1,0:T(8,128)S(1)} %copy-done, ...), custom_call_target="tpu_custom_call" | custom-call | flops 1048576 | bytes 8388608 | tf_op jit(solution)/shard_map/pallas_call | solution.py:72
  25.8 3.9 %collective-permute-start.5 = (bf16[4,137,256]{2,1,0:T(8,128)(2,1)S(1)}, bf16[4,137,256]{2,1,0:T(8,128)(2,1)S(1)}, u32[]{:S(2)}, u32[]{:S(2)}) collective-permute-start(bf16[4,137,256]{2,1,0:T(8,128)(2,1)S(1)} %collective-permute-done.3.inc), channel_id=1, source_target_pairs={{0,4},{1,5},{2,0},{3,1},{6,2},{7,3},{4,6},{5,7},{8,12},{9,13},{10,... | collective-permute-start | bytes 841736 | tf_op jit(solution)/shard_map/ppermute | solution.py:209
  29.7 0.0 collective-permute-start.4
  29.7 3.1 %shard_map.76 = s16[4,144,256]{2,1,0:T(8,128)(2,1)S(1)} custom-call(s32[112]{0:T(128)S(1)} %pad_add_fusion.table, bf16[4,137,256]{2,1,0:T(8,128)(2,1)S(1)} %collective-permute-done.3.inc, bf16[96,137,128]{2,1,0:T(8,128)(2,1)S(1)} %get-tuple-element.30.jac, bf16[96,128,256]{2,1,0:T(8,128)(2,1)S(1)} %get-tuple-element.31.inn, s32[96,256]{1,0:T(8,128)S(1)} %copy-done, ...), custom_call_target="tpu_custom_call" | custom-call | flops 1048576 | bytes 8388608 | tf_op jit(solution)/shard_map/pallas_call | solution.py:72
  32.8 0.0 collective-permute-done.7.inc
  32.8 3.1 %shard_map.77 = s16[4,144,256]{2,1,0:T(8,128)(2,1)S(1)} custom-call(s32[112]{0:T(128)S(1)} %pad_add_fusion.table, bf16[4,137,256]{2,1,0:T(8,128)(2,1)S(1)} %collective-permute-done.7.inc, bf16[96,137,128]{2,1,0:T(8,128)(2,1)S(1)} %get-tuple-element.30.jac, bf16[96,128,256]{2,1,0:T(8,128)(2,1)S(1)} %get-tuple-element.31.inn, s32[96,256]{1,0:T(8,128)S(1)} %copy-done, ...), custom_call_target="tpu_custom_call" | custom-call | flops 1048576 | bytes 8388608 | tf_op jit(solution)/shard_map/pallas_call | solution.py:72
  35.9 0.1 collective-permute-start.9
  36.0 0.0 collective-permute-done.6.inc
  36.0 0.0 collective-permute-done.5.inc
  36.0 1.3 %shard_map.78 = s16[4,144,256]{2,1,0:T(8,128)(2,1)S(1)} custom-call(s32[112]{0:T(128)S(1)} %pad_add_fusion.table, bf16[4,137,256]{2,1,0:T(8,128)(2,1)S(1)} %collective-permute-done.5.inc, bf16[96,137,128]{2,1,0:T(8,128)(2,1)S(1)} %get-tuple-element.30.jac, bf16[96,128,256]{2,1,0:T(8,128)(2,1)S(1)} %get-tuple-element.31.inn, s32[96,256]{1,0:T(8,128)S(1)} %copy-done, ...), custom_call_target="tpu_custom_call" | custom-call | flops 1048576 | bytes 8388608 | tf_op jit(solution)/shard_map/pallas_call | solution.py:72
  37.3 2.7 %collective-permute-start.12 = (s16[4,144,256]{2,1,0:T(8,128)(2,1)S(1)}, s16[4,144,256]{2,1,0:T(8,128)(2,1)S(1)}, u32[]{:S(2)}, u32[]{:S(2)}) collective-permute-start(s16[4,144,256]{2,1,0:T(8,128)(2,1)S(1)} %shard_map.78), channel_id=1, source_target_pairs={{0,1},{1,0},{2,3},{3,2},{4,5},{5,4},{6,7},{7,6},{8,9},{9,8},{10,11... | collective-permute-start | bytes 884744 | tf_op jit(solution)/shard_map/ppermute | solution.py:212
  40.0 0.0 collective-permute-done.4.refs_0_
  40.0 1.9 %shard_map.79 = s16[4,144,256]{2,1,0:T(8,128)(2,1)S(1)} custom-call(s32[112]{0:T(128)S(1)} %pad_add_fusion.table, bf16[4,137,256]{2,1,0:T(8,128)(2,1)S(1)} %collective-permute-done.inc, bf16[96,137,128]{2,1,0:T(8,128)(2,1)S(1)} %get-tuple-element.30.jac, bf16[96,128,256]{2,1,0:T(8,128)(2,1)S(1)} %get-tuple-element.31.inn, s32[96,256]{1,0:T(8,128)S(1)} %copy-done, ...), custom_call_target="tpu_custom_call" | custom-call | flops 1048576 | bytes 8388608 | tf_op jit(solution)/shard_map/pallas_call | solution.py:72
  41.9 0.2 collective-permute-start.8
  42.2 3.8 %collective-permute-done.9.refs_0_ = s16[4,144,256]{2,1,0:T(8,128)(2,1)S(1)} collective-permute-done((s16[4,144,256]{2,1,0:T(8,128)(2,1)S(1)}, s16[4,144,256]{2,1,0:T(8,128)(2,1)S(1)}, u32[]{:S(2)}, u32[]{:S(2)}) %collective-permute-start.9) | collective-permute-done | bytes 294944 | tf_op jit(solution)/shard_map/ppermute | solution.py:212
  45.9 1.3 %shard_map.80 = s16[4,144,256]{2,1,0:T(8,128)(2,1)S(1)} custom-call(s32[112]{0:T(128)S(1)} %pad_add_fusion.table, bf16[4,137,256]{2,1,0:T(8,128)(2,1)S(1)} %collective-permute-done.2.inc, bf16[96,137,128]{2,1,0:T(8,128)(2,1)S(1)} %get-tuple-element.30.jac, bf16[96,128,256]{2,1,0:T(8,128)(2,1)S(1)} %get-tuple-element.31.inn, s32[96,256]{1,0:T(8,128)S(1)} %copy-done, ...), custom_call_target="tpu_custom_call" | custom-call | flops 1048576 | bytes 8388608 | tf_op jit(solution)/shard_map/pallas_call | solution.py:72
  47.3 2.8 %collective-permute-start.10 = (s16[4,144,256]{2,1,0:T(8,128)(2,1)S(1)}, s16[4,144,256]{2,1,0:T(8,128)(2,1)S(1)}, u32[]{:S(2)}, u32[]{:S(2)}) collective-permute-start(s16[4,144,256]{2,1,0:T(8,128)(2,1)S(1)} %shard_map.80), channel_id=1, source_target_pairs={{0,6},{1,7},{2,4},{3,5},{6,0},{7,1},{4,2},{5,3},{8,14},{9,15},{10,... | collective-permute-start | bytes 884744 | tf_op jit(solution)/shard_map/ppermute | solution.py:209
  50.0 1.0 %collective-permute-start.11 = (s16[4,144,256]{2,1,0:T(8,128)(2,1)S(1)}, s16[4,144,256]{2,1,0:T(8,128)(2,1)S(1)}, u32[]{:S(2)}, u32[]{:S(2)}) collective-permute-start(s16[4,144,256]{2,1,0:T(8,128)(2,1)S(1)} %shard_map.76), channel_id=1, source_target_pairs={{0,1},{1,0},{2,3},{3,2},{4,5},{5,4},{6,7},{7,6},{8,9},{9,8},{10,11... | collective-permute-start | bytes 884744 | tf_op jit(solution)/shard_map/ppermute | solution.py:212
  51.1 0.0 collective-permute-done.12.refs_0_
  51.1 1.9 %shard_map.81 = s16[4,144,256]{2,1,0:T(8,128)(2,1)S(1)} custom-call(s32[112]{0:T(128)S(1)} %pad_add_fusion.table, bf16[4,137,256]{2,1,0:T(8,128)(2,1)S(1)} %collective-permute-done.6.inc, bf16[96,137,128]{2,1,0:T(8,128)(2,1)S(1)} %get-tuple-element.30.jac, bf16[96,128,256]{2,1,0:T(8,128)(2,1)S(1)} %get-tuple-element.31.inn, s32[96,256]{1,0:T(8,128)S(1)} %copy-done, ...), custom_call_target="tpu_custom_call" | custom-call | flops 1048576 | bytes 8388608 | tf_op jit(solution)/shard_map/pallas_call | solution.py:72
  53.0 0.9 %collective-permute-start.13 = (s16[4,144,256]{2,1,0:T(8,128)(2,1)S(1)}, s16[4,144,256]{2,1,0:T(8,128)(2,1)S(1)}, u32[]{:S(2)}, u32[]{:S(2)}) collective-permute-start(s16[4,144,256]{2,1,0:T(8,128)(2,1)S(1)} %shard_map.81), channel_id=1, source_target_pairs={{0,2},{1,3},{2,6},{3,7},{6,4},{7,5},{4,0},{5,1},{8,10},{9,11},{10,... | collective-permute-start | bytes 884744 | tf_op jit(solution)/shard_map/ppermute | solution.py:209
  53.9 0.0 collective-permute-done.8.refs_0_
  53.9 4.7 %collective-permute-done.10.refs_1_ = s16[4,144,256]{2,1,0:T(8,128)(2,1)S(1)} collective-permute-done((s16[4,144,256]{2,1,0:T(8,128)(2,1)S(1)}, s16[4,144,256]{2,1,0:T(8,128)(2,1)S(1)}, u32[]{:S(2)}, u32[]{:S(2)}) %collective-permute-start.10) | collective-permute-done | bytes 294944 | tf_op jit(solution)/shard_map/ppermute | solution.py:209
  58.6 0.0 collective-permute-done.11.refs_2_
  58.6 9.4 %collective-permute-done.13.refs_3_ = s16[4,144,256]{2,1,0:T(8,128)(2,1)S(1)} collective-permute-done((s16[4,144,256]{2,1,0:T(8,128)(2,1)S(1)}, s16[4,144,256]{2,1,0:T(8,128)(2,1)S(1)}, u32[]{:S(2)}, u32[]{:S(2)}) %collective-permute-start.13) | collective-permute-done | bytes 294944 | tf_op jit(solution)/shard_map/ppermute | solution.py:209
  68.0 1.3 %shard_map.82 = f32[137,4,256]{2,1,0:T(4,128)} custom-call(f32[4,137,256]{2,1,0:T(8,128)S(1)} %shard_map.74.own, s16[4,144,256]{2,1,0:T(8,128)(2,1)S(1)} %collective-permute-done.8.refs_0_, s16[4,144,256]{2,1,0:T(8,128)(2,1)S(1)} %collective-permute-done.10.refs_1_, s16[4,144,256]{2,1,0:T(8,128)(2,1)S(1)} %collective-permute-done.11.refs_2_, ...), custom_call_target="tpu_custom_call" | custom-call | flops 1048576 | bytes 8388608 | tf_op jit(solution)/shard_map/pallas_call | solution.py:165
  (1 shorter events, 0.0 us)
Async XLA Ops:
  0.0 15.0 %copy-start = (s32[96,256]{1,0:T(8,128)S(1)}, s32[96,256]{1,0:T(8,128)}, u32[]{:S(2)}) copy-start(s32[96,256]{1,0:T(8,128)} %cnt.15) | copy-start | bytes 294916
  1.0 15.2 %collective-permute-start.3 = (bf16[4,137,256]{2,1,0:T(8,128)(2,1)S(1)}, bf16[4,137,256]{2,1,0:T(8,128)(2,1)S(1)}, u32[]{:S(2)}, u32[]{:S(2)}) collective-permute-start(bf16[4,137,256]{2,1,0:T(8,128)(2,1)S(1)} %copy.12.inc), channel_id=1, source_target_pairs={{0,1},{1,0},{2,3},{3,2},{4,5},{5,4},{6,7},{7,6},{8,9},{9,8},{10,11... | collective-permute-start | bytes 841736 | tf_op jit(solution)/shard_map/ppermute | solution.py:212
  4.1 9.4 %collective-permute-start = (bf16[4,137,256]{2,1,0:T(8,128)(2,1)S(1)}, bf16[4,137,256]{2,1,0:T(8,128)(2,1)S(1)}, u32[]{:S(2)}, u32[]{:S(2)}) collective-permute-start(bf16[4,137,256]{2,1,0:T(8,128)(2,1)S(1)} %copy.12.inc), channel_id=1, source_target_pairs={{0,2},{1,3},{2,6},{3,7},{6,4},{7,5},{4,0},{5,1},{8,10},{9,11},{10,... | collective-permute-start | bytes 841736 | tf_op jit(solution)/shard_map/ppermute | solution.py:209
  13.4 8.5 %collective-permute-start.2 = (bf16[4,137,256]{2,1,0:T(8,128)(2,1)S(1)}, bf16[4,137,256]{2,1,0:T(8,128)(2,1)S(1)}, u32[]{:S(2)}, u32[]{:S(2)}) collective-permute-start(bf16[4,137,256]{2,1,0:T(8,128)(2,1)S(1)} %collective-permute-done.inc), channel_id=1, source_target_pairs={{0,2},{1,3},{2,6},{3,7},{6,4},{7,5},{4,0},{5,1},{8,10},{9,11},{10,... | collective-permute-start | bytes 841736 | tf_op jit(solution)/shard_map/ppermute | solution.py:209
  14.2 9.7 %collective-permute-start.1 = (bf16[4,137,256]{2,1,0:T(8,128)(2,1)S(1)}, bf16[4,137,256]{2,1,0:T(8,128)(2,1)S(1)}, u32[]{:S(2)}, u32[]{:S(2)}) collective-permute-start(bf16[4,137,256]{2,1,0:T(8,128)(2,1)S(1)} %collective-permute-done.inc), channel_id=1, source_target_pairs={{0,1},{1,0},{2,3},{3,2},{4,5},{5,4},{6,7},{7,6},{8,9},{9,8},{10,11... | collective-permute-start | bytes 841736 | tf_op jit(solution)/shard_map/ppermute | solution.py:212
  21.9 10.9 %collective-permute-start.7 = (bf16[4,137,256]{2,1,0:T(8,128)(2,1)S(1)}, bf16[4,137,256]{2,1,0:T(8,128)(2,1)S(1)}, u32[]{:S(2)}, u32[]{:S(2)}) collective-permute-start(bf16[4,137,256]{2,1,0:T(8,128)(2,1)S(1)} %collective-permute-done.2.inc), channel_id=1, source_target_pairs={{0,1},{1,0},{2,3},{3,2},{4,5},{5,4},{6,7},{7,6},{8,9},{9,8},{10,11... | collective-permute-start | bytes 841736 | tf_op jit(solution)/shard_map/ppermute | solution.py:212
  22.7 13.3 %collective-permute-start.6 = (bf16[4,137,256]{2,1,0:T(8,128)(2,1)S(1)}, bf16[4,137,256]{2,1,0:T(8,128)(2,1)S(1)}, u32[]{:S(2)}, u32[]{:S(2)}) collective-permute-start(bf16[4,137,256]{2,1,0:T(8,128)(2,1)S(1)} %copy.12.inc), channel_id=1, source_target_pairs={{0,4},{1,5},{2,0},{3,1},{6,2},{7,3},{4,6},{5,7},{8,12},{9,13},{10,... | collective-permute-start | bytes 841736 | tf_op jit(solution)/shard_map/ppermute | solution.py:209
  25.8 10.2 %collective-permute-start.5 = (bf16[4,137,256]{2,1,0:T(8,128)(2,1)S(1)}, bf16[4,137,256]{2,1,0:T(8,128)(2,1)S(1)}, u32[]{:S(2)}, u32[]{:S(2)}) collective-permute-start(bf16[4,137,256]{2,1,0:T(8,128)(2,1)S(1)} %collective-permute-done.3.inc), channel_id=1, source_target_pairs={{0,4},{1,5},{2,0},{3,1},{6,2},{7,3},{4,6},{5,7},{8,12},{9,13},{10,... | collective-permute-start | bytes 841736 | tf_op jit(solution)/shard_map/ppermute | solution.py:209
  29.7 10.3 %collective-permute-start.4 = (s16[4,144,256]{2,1,0:T(8,128)(2,1)S(1)}, s16[4,144,256]{2,1,0:T(8,128)(2,1)S(1)}, u32[]{:S(2)}, u32[]{:S(2)}) collective-permute-start(s16[4,144,256]{2,1,0:T(8,128)(2,1)S(1)} %shard_map.75), channel_id=1, source_target_pairs={{0,1},{1,0},{2,3},{3,2},{4,5},{5,4},{6,7},{7,6},{8,9},{9,8},{10,11... | collective-permute-start | bytes 884744 | tf_op jit(solution)/shard_map/ppermute | solution.py:212
  35.9 10.0 %collective-permute-start.9 = (s16[4,144,256]{2,1,0:T(8,128)(2,1)S(1)}, s16[4,144,256]{2,1,0:T(8,128)(2,1)S(1)}, u32[]{:S(2)}, u32[]{:S(2)}) collective-permute-start(s16[4,144,256]{2,1,0:T(8,128)(2,1)S(1)} %shard_map.77), channel_id=1, source_target_pairs={{0,1},{1,0},{2,3},{3,2},{4,5},{5,4},{6,7},{7,6},{8,9},{9,8},{10,11... | collective-permute-start | bytes 884744 | tf_op jit(solution)/shard_map/ppermute | solution.py:212
  37.3 13.7 %collective-permute-start.12 = (s16[4,144,256]{2,1,0:T(8,128)(2,1)S(1)}, s16[4,144,256]{2,1,0:T(8,128)(2,1)S(1)}, u32[]{:S(2)}, u32[]{:S(2)}) collective-permute-start(s16[4,144,256]{2,1,0:T(8,128)(2,1)S(1)} %shard_map.78), channel_id=1, source_target_pairs={{0,1},{1,0},{2,3},{3,2},{4,5},{5,4},{6,7},{7,6},{8,9},{9,8},{10,11... | collective-permute-start | bytes 884744 | tf_op jit(solution)/shard_map/ppermute | solution.py:212
  41.9 12.0 %collective-permute-start.8 = (s16[4,144,256]{2,1,0:T(8,128)(2,1)S(1)}, s16[4,144,256]{2,1,0:T(8,128)(2,1)S(1)}, u32[]{:S(2)}, u32[]{:S(2)}) collective-permute-start(s16[4,144,256]{2,1,0:T(8,128)(2,1)S(1)} %shard_map.79), channel_id=1, source_target_pairs={{0,4},{1,5},{2,0},{3,1},{6,2},{7,3},{4,6},{5,7},{8,12},{9,13},{10,... | collective-permute-start | bytes 884744 | tf_op jit(solution)/shard_map/ppermute | solution.py:209
  47.3 11.3 %collective-permute-start.10 = (s16[4,144,256]{2,1,0:T(8,128)(2,1)S(1)}, s16[4,144,256]{2,1,0:T(8,128)(2,1)S(1)}, u32[]{:S(2)}, u32[]{:S(2)}) collective-permute-start(s16[4,144,256]{2,1,0:T(8,128)(2,1)S(1)} %shard_map.80), channel_id=1, source_target_pairs={{0,6},{1,7},{2,4},{3,5},{6,0},{7,1},{4,2},{5,3},{8,14},{9,15},{10,... | collective-permute-start | bytes 884744 | tf_op jit(solution)/shard_map/ppermute | solution.py:209
  50.0 8.6 %collective-permute-start.11 = (s16[4,144,256]{2,1,0:T(8,128)(2,1)S(1)}, s16[4,144,256]{2,1,0:T(8,128)(2,1)S(1)}, u32[]{:S(2)}, u32[]{:S(2)}) collective-permute-start(s16[4,144,256]{2,1,0:T(8,128)(2,1)S(1)} %shard_map.76), channel_id=1, source_target_pairs={{0,1},{1,0},{2,3},{3,2},{4,5},{5,4},{6,7},{7,6},{8,9},{9,8},{10,11... | collective-permute-start | bytes 884744 | tf_op jit(solution)/shard_map/ppermute | solution.py:212
  53.0 15.0 %collective-permute-start.13 = (s16[4,144,256]{2,1,0:T(8,128)(2,1)S(1)}, s16[4,144,256]{2,1,0:T(8,128)(2,1)S(1)}, u32[]{:S(2)}, u32[]{:S(2)}) collective-permute-start(s16[4,144,256]{2,1,0:T(8,128)(2,1)S(1)} %shard_map.81), channel_id=1, source_target_pairs={{0,2},{1,3},{2,6},{3,7},{6,4},{7,5},{4,0},{5,1},{8,10},{9,11},{10,... | collective-permute-start | bytes 884744 | tf_op jit(solution)/shard_map/ppermute | solution.py:209
